TPU v7x, 32 devices: a whole 2x2x4 slice. The times are simulated.
32 devices in a mesh: replica: 8 (over y, x, core), group: 4 (over z).
Axes of the slice: x: 2, y: 2, z: 4, core: 2. Of those that a mesh axis runs over, the one named last changes fastest.
Arguments:
- layer_input: bfloat16 [8192, 1024], P(('replica', 'group')), may hold values from -6 to 6
- qkv_weight: bfloat16 [1024, 3072], P('group'), may hold values from -0.1875 to 0.1875
- query_bias: bfloat16 [1024], P('group'), may hold values from -3 to 3
- value_bias: bfloat16 [1024], P('group'), may hold values from -3 to 3
- attn_weight: bfloat16 [1024, 1024], P('group'), may hold values from -0.5 to 0.5
- attn_bias: bfloat16 [1024], P('group'), may hold values from -1.75 to 1.75
- first_gain: bfloat16 [1024], P('group'), may hold values from 0.5 to 1.5
- first_shift: bfloat16 [1024], P('group'), may hold values from -1.75 to 1.75
- inner_weight: bfloat16 [1024, 4096], P('group'), may hold values from -0.1875 to 0.1875
- inner_bias: bfloat16 [4096], P('group'), may hold values from -3 to 3
- outer_weight: bfloat16 [4096, 1024], P('group'), may hold values from -0.09375 to 0.09375
- outer_bias: bfloat16 [1024], P('group'), may hold values from -1.75 to 1.75
- second_gain: bfloat16 [1024], P('group'), may hold values from 0.5 to 1.5
- second_shift: bfloat16 [1024], P('group'), may hold values from -1.75 to 1.75
- segment_ids: int32 [8192], P('replica'), may hold values from 0 to 6, as said below
- output_grad: bfloat16 [8192, 1024], P(('replica', 'group')), may hold values from -6 to 6
Outputs:
- layer_output: bfloat16 [8192, 1024], P(('replica', 'group'))
- input_grad: bfloat16 [8192, 1024], P(('replica', 'group'))
- qkv_weight_grad: float32 [1024, 3072], P('group')
- query_bias_grad: float32 [1024], P('group')
- value_bias_grad: float32 [1024], P('group')
- attn_weight_grad: float32 [1024, 1024], P('group')
- attn_bias_grad: float32 [1024], P('group')
- first_gain_grad: float32 [1024], P('group')
- first_shift_grad: float32 [1024], P('group')
- inner_weight_grad: float32 [1024, 4096], P('group')
- inner_bias_grad: float32 [4096], P('group')
- outer_weight_grad: float32 [4096, 1024], P('group')
- outer_bias_grad: float32 [1024], P('group')
- second_gain_grad: float32 [1024], P('group')
- second_shift_grad: float32 [1024], P('group')
Inputs may be any that keep to these rules, and one draw needn't show every extreme that they name: `segment_ids`: within each aligned run of 1024 tokens the ids never fall; tokens of different runs never attend to each other.
All inputs are finite; a program needn't handle non-finite values.
Results may differ from a plain program's by a relative error of at most 0.02.
Values may be sent and summed in bfloat16 or wider, within the bound.
A program may use at most 192 MiB of HBM per device.

v0:
```python
import jax
import jax.numpy as jnp
from jax import lax
from jax.sharding import PartitionSpec as P

D = 1024
HEADS = 16
HD = 64


NORM_EPS = 1e-05


def layer_norm(resid, gain, shift):
    average = jnp.mean(resid, axis=-1, keepdims=True)
    centred = resid - average
    variance = jnp.mean(centred * centred, axis=-1, keepdims=True)
    return centred * lax.rsqrt(variance + NORM_EPS) * gain + shift


def gelu_exact(values):
    return jax.nn.gelu(values, approximate=False)


def matmul(left, right):
    return jnp.dot(left, right, preferred_element_type=jnp.float32)


def on_device(
    layer_input,
    qkv_weight,
    query_bias,
    value_bias,
    attn_weight,
    attn_bias,
    first_gain,
    first_shift,
    inner_weight,
    inner_bias,
    outer_weight,
    outer_bias,
    second_gain,
    second_shift,
    segment_ids,
    output_grad,
):
    whole = (
        lax.all_gather(qkv_weight, "group", axis=0, tiled=True),
        lax.all_gather(query_bias, "group", axis=0, tiled=True),
        lax.all_gather(value_bias, "group", axis=0, tiled=True),
        lax.all_gather(attn_weight, "group", axis=0, tiled=True),
        lax.all_gather(attn_bias, "group", axis=0, tiled=True),
        lax.all_gather(first_gain, "group", axis=0, tiled=True),
        lax.all_gather(first_shift, "group", axis=0, tiled=True),
        lax.all_gather(inner_weight, "group", axis=0, tiled=True),
        lax.all_gather(inner_bias, "group", axis=0, tiled=True),
        lax.all_gather(outer_weight, "group", axis=0, tiled=True),
        lax.all_gather(outer_bias, "group", axis=0, tiled=True),
        lax.all_gather(second_gain, "group", axis=0, tiled=True),
        lax.all_gather(second_shift, "group", axis=0, tiled=True),
    )
    (
        qkv_full,
        query_full,
        value_full,
        attn_full,
        attn_bias_full,
        gain_one,
        shift_one,
        inner_full,
        inner_bias_full,
        outer_full,
        outer_bias_full,
        gain_two,
        shift_two,
    ) = whole
    row_count = layer_input.shape[0]
    length = segment_ids.shape[0]
    group_place = lax.axis_index("group")
    score_scale = HD ** (-0.5)
    projected = matmul(layer_input, qkv_full)
    queries = ((projected[:, :D] + query_full) * score_scale).astype(jnp.bfloat16)
    key_rows = projected[:, D : 2 * D].astype(jnp.bfloat16)
    value_rows = (projected[:, 2 * D :] + value_full).astype(jnp.bfloat16)
    key_all, value_all = (
        lax.all_gather(key_rows, "group", axis=0, tiled=True),
        lax.all_gather(value_rows, "group", axis=0, tiled=True),
    )
    own_ids = lax.dynamic_slice_in_dim(segment_ids, group_place * row_count, row_count)
    allowed = own_ids[:, None] == segment_ids[None, :]
    query_heads = queries.reshape(row_count, HEADS, HD)
    key_heads = key_all.reshape(length, HEADS, HD)
    value_heads = value_all.reshape(length, HEADS, HD)

    def masked_scores():
        raw = jnp.einsum("qhd,khd->hqk", query_heads, key_heads, preferred_element_type=jnp.float32)
        return jnp.where(allowed[None], raw, -1e30)

    scores = masked_scores()
    row_peak = jnp.max(scores, axis=-1, keepdims=True)
    exponent = jnp.exp(scores - row_peak)
    row_total = jnp.sum(exponent, axis=-1, keepdims=True)
    log_total = row_peak + jnp.log(row_total)
    attn_probs = (exponent / row_total).astype(jnp.bfloat16)
    attended = jnp.einsum(
        "hqk,khd->qhd", attn_probs, value_heads, preferred_element_type=jnp.float32
    )
    attended = attended.reshape(row_count, D).astype(jnp.bfloat16)
    branch = matmul(attended, attn_full) + attn_bias_full
    residual_one = layer_input.astype(jnp.float32) + branch
    first, first_pull = jax.vjp(
        layer_norm, residual_one, gain_one.astype(jnp.float32), shift_one.astype(jnp.float32)
    )
    first_low = first.astype(jnp.bfloat16)
    inner = matmul(first_low, inner_full) + inner_bias_full
    activated_f, gelu_pull = jax.vjp(gelu_exact, inner)
    activated = activated_f.astype(jnp.bfloat16)
    outer = matmul(activated, outer_full) + outer_bias_full
    result, second_pull = jax.vjp(
        layer_norm, first + outer, gain_two.astype(jnp.float32), shift_two.astype(jnp.float32)
    )
    layer_output = result.astype(jnp.bfloat16)
    qkv_back, attn_back, inner_back, outer_back = (
        lax.all_gather(qkv_weight, "group", axis=0, tiled=True),
        lax.all_gather(attn_weight, "group", axis=0, tiled=True),
        lax.all_gather(inner_weight, "group", axis=0, tiled=True),
        lax.all_gather(outer_weight, "group", axis=0, tiled=True),
    )
    second_res_grad, second_gain_grad, second_shift_grad = second_pull(
        output_grad.astype(jnp.float32)
    )
    outer_grad = second_res_grad.astype(jnp.bfloat16)
    outer_bias_grad = jnp.sum(outer_grad.astype(jnp.float32), axis=0)
    inner_grad = gelu_pull(matmul(outer_grad, outer_back.T))[0].astype(jnp.bfloat16)
    inner_bias_grad = jnp.sum(inner_grad.astype(jnp.float32), axis=0)
    first_grad = second_res_grad + matmul(inner_grad, inner_back.T)
    first_res_grad, first_gain_grad, first_shift_grad = first_pull(first_grad)
    branch_grad = first_res_grad.astype(jnp.bfloat16)
    attn_bias_grad = jnp.sum(branch_grad.astype(jnp.float32), axis=0)
    attended_grad = (
        matmul(branch_grad, attn_back.T).astype(jnp.bfloat16).reshape(row_count, HEADS, HD)
    )
    probs = jnp.exp(masked_scores() - log_total)
    probs_low = probs.astype(jnp.bfloat16)
    probs_grad = jnp.einsum(
        "qhd,khd->hqk", attended_grad, value_heads, preferred_element_type=jnp.float32
    )
    value_terms = jnp.einsum(
        "hqk,qhd->khd", probs_low, attended_grad, preferred_element_type=jnp.float32
    )
    weighted = jnp.sum(probs * probs_grad, axis=-1, keepdims=True)
    scores_grad = (probs * (probs_grad - weighted)).astype(jnp.bfloat16)
    queries_grad = jnp.einsum(
        "hqk,khd->qhd", scores_grad, key_heads, preferred_element_type=jnp.float32
    )
    queries_grad = queries_grad.reshape(row_count, D).astype(jnp.bfloat16)
    key_terms = jnp.einsum(
        "hqk,qhd->khd", scores_grad, query_heads, preferred_element_type=jnp.float32
    )
    keys_grad, values_grad = (
        lax.psum_scatter(
            key_terms.reshape(length, D).astype(jnp.bfloat16),
            "group",
            scatter_dimension=0,
            tiled=True,
        ).astype(jnp.float32),
        lax.psum_scatter(
            value_terms.reshape(length, D).astype(jnp.bfloat16),
            "group",
            scatter_dimension=0,
            tiled=True,
        ).astype(jnp.float32),
    )
    keys_grad = keys_grad.astype(jnp.bfloat16)
    values_grad = values_grad.astype(jnp.bfloat16)
    scaled_queries = (queries_grad.astype(jnp.float32) * score_scale).astype(jnp.bfloat16)
    projected_grad = jnp.concatenate([scaled_queries, keys_grad, values_grad], axis=1)
    query_bias_grad = jnp.sum(scaled_queries.astype(jnp.float32), axis=0)
    value_bias_grad = jnp.sum(values_grad.astype(jnp.float32), axis=0)
    input_grad = (first_res_grad + matmul(projected_grad, qkv_back.T)).astype(jnp.bfloat16)
    proj_all, branch_all, inner_all, outer_all = (
        lax.all_gather(projected_grad, "group", axis=0, tiled=True),
        lax.all_gather(branch_grad, "group", axis=0, tiled=True),
        lax.all_gather(inner_grad, "group", axis=0, tiled=True),
        lax.all_gather(outer_grad, "group", axis=0, tiled=True),
    )
    input_cols, attended_cols, first_cols, activated_cols = (
        lax.all_to_all(layer_input, "group", split_axis=1, concat_axis=0, tiled=True),
        lax.all_to_all(attended, "group", split_axis=1, concat_axis=0, tiled=True),
        lax.all_to_all(first_low, "group", split_axis=1, concat_axis=0, tiled=True),
        lax.all_to_all(activated, "group", split_axis=1, concat_axis=0, tiled=True),
    )
    vectors = (
        lax.psum_scatter(
            query_bias_grad.astype(jnp.bfloat16), "group", scatter_dimension=0, tiled=True
        ).astype(jnp.float32),
        lax.psum_scatter(
            value_bias_grad.astype(jnp.bfloat16), "group", scatter_dimension=0, tiled=True
        ).astype(jnp.float32),
        lax.psum_scatter(
            attn_bias_grad.astype(jnp.bfloat16), "group", scatter_dimension=0, tiled=True
        ).astype(jnp.float32),
        lax.psum_scatter(
            first_gain_grad.astype(jnp.bfloat16), "group", scatter_dimension=0, tiled=True
        ).astype(jnp.float32),
        lax.psum_scatter(
            first_shift_grad.astype(jnp.bfloat16), "group", scatter_dimension=0, tiled=True
        ).astype(jnp.float32),
        lax.psum_scatter(
            inner_bias_grad.astype(jnp.bfloat16), "group", scatter_dimension=0, tiled=True
        ).astype(jnp.float32),
        lax.psum_scatter(
            outer_bias_grad.astype(jnp.bfloat16), "group", scatter_dimension=0, tiled=True
        ).astype(jnp.float32),
        lax.psum_scatter(
            second_gain_grad.astype(jnp.bfloat16), "group", scatter_dimension=0, tiled=True
        ).astype(jnp.float32),
        lax.psum_scatter(
            second_shift_grad.astype(jnp.bfloat16), "group", scatter_dimension=0, tiled=True
        ).astype(jnp.float32),
    )
    owned = (
        matmul(input_cols.T, proj_all),
        vectors[0],
        vectors[1],
        matmul(attended_cols.T, branch_all),
        vectors[2],
        vectors[3],
        vectors[4],
        matmul(first_cols.T, inner_all),
        vectors[5],
        matmul(activated_cols.T, outer_all),
        vectors[6],
        vectors[7],
        vectors[8],
    )
    summed = (
        lax.psum(owned[0].astype(jnp.bfloat16), "replica").astype(jnp.float32),
        lax.psum(owned[1].astype(jnp.bfloat16), "replica").astype(jnp.float32),
        lax.psum(owned[2].astype(jnp.bfloat16), "replica").astype(jnp.float32),
        lax.psum(owned[3].astype(jnp.bfloat16), "replica").astype(jnp.float32),
        lax.psum(owned[4].astype(jnp.bfloat16), "replica").astype(jnp.float32),
        lax.psum(owned[5].astype(jnp.bfloat16), "replica").astype(jnp.float32),
        lax.psum(owned[6].astype(jnp.bfloat16), "replica").astype(jnp.float32),
        lax.psum(owned[7].astype(jnp.bfloat16), "replica").astype(jnp.float32),
        lax.psum(owned[8].astype(jnp.bfloat16), "replica").astype(jnp.float32),
        lax.psum(owned[9].astype(jnp.bfloat16), "replica").astype(jnp.float32),
        lax.psum(owned[10].astype(jnp.bfloat16), "replica").astype(jnp.float32),
        lax.psum(owned[11].astype(jnp.bfloat16), "replica").astype(jnp.float32),
        lax.psum(owned[12].astype(jnp.bfloat16), "replica").astype(jnp.float32),
    )
    return (
        layer_output,
        input_grad,
        summed[0],
        summed[1],
        summed[2],
        summed[3],
        summed[4],
        summed[5],
        summed[6],
        summed[7],
        summed[8],
        summed[9],
        summed[10],
        summed[11],
        summed[12],
    )


def solution(mesh):
    in_specs = (
        P(("replica", "group"), None),
        P("group", None),
        P("group"),
        P("group"),
        P("group", None),
        P("group"),
        P("group"),
        P("group"),
        P("group", None),
        P("group"),
        P("group", None),
        P("group"),
        P("group"),
        P("group"),
        P("replica"),
        P(("replica", "group"), None),
    )
    out_specs = (
        P(("replica", "group"), None),
        P(("replica", "group"), None),
        P("group", None),
        P("group"),
        P("group"),
        P("group", None),
        P("group"),
        P("group"),
        P("group"),
        P("group", None),
        P("group"),
        P("group", None),
        P("group"),
        P("group"),
        P("group"),
    )
    return jax.shard_map(
        on_device, mesh=mesh, in_specs=in_specs, out_specs=out_specs, check_vma=False
    )
```

profile of v0, /device:TPU:0, one launch (start us, length us, event | category | flops | bytes accessed | tf_op | source)
XLA Modules:
  0.0 1246.2 jit_solution(6549477570825857560)
XLA Ops:
  8.6 12.6 %all-gather.1 = bf16[4,1,256]{2,1,0:T(2,128)(2,1)S(1)} all-gather(bf16[1,1,256]{2,1,0:T(2,128)(2,1)S(1)} %reshape.182), channel_id=1, replica_groups=mesh['replica'=8,'group'=4] {'group'}, dimensions={0}, use_global_device_ids=true | all-gather | bytes 2560 | tf_op jit(solution)/shard_map/all_gather | solution.py:49
  21.9 7.8 all-gather
  29.7 97.9 %all-gather.19.cloned.1.call-done = bf16[1024,3072]{1,0:T(8,128)(2,1)} async-done(((bf16[256,3072]{1,0:T(8,128)(2,1)}), bf16[1024,3072]{1,0:T(8,128)(2,1)}) %all-gather.19.cloned.1.call-update) | async-done | bytes 6291472 | tf_op jit(solution)/shard_map/all_gather | solution.py:48
  127.6 4.8 fusion.46
  136.5 8.0 all-gather.5
  144.5 11.9 all_gather.71
  156.5 8.4 all-gather.2
  165.0 9.0 all-gather.4
  174.0 8.1 all-gather.3
  182.2 9.1 all-gather.6
  191.3 8.2 all-gather.7
  200.1 4.1 copy.58
  204.2 21.1 %all-gather.23.cloned.1.call-done = bf16[1024,1024]{1,0:T(8,128)(2,1)} async-done(((bf16[256,1024]{1,0:T(8,128)(2,1)}), bf16[1024,1024]{1,0:T(8,128)(2,1)}) %all-gather.23.cloned.1.call-update) | async-done | bytes 2097168 | tf_op jit(solution)/shard_map/all_gather | solution.py:86
  230.9 3.9 fusion
  237.4 5.4 fusion.24
  242.8 28.6 %all-gather.25.cloned.1.call-done = bf16[1024,1024]{1,0:T(8,128)(2,1)} async-done(((bf16[256,1024]{1,0:T(8,128)(2,1)}), bf16[1024,1024]{1,0:T(8,128)(2,1)}) %all-gather.25.cloned.1.call-update) | async-done | bytes 2097168 | tf_op jit(solution)/shard_map/all_gather | solution.py:51
  275.4 146.0 %all-gather.27.cloned.1.call-done = bf16[1024,4096]{1,0:T(8,128)(2,1)} async-done(((bf16[256,4096]{1,0:T(8,128)(2,1)}), bf16[1024,4096]{1,0:T(8,128)(2,1)}) %all-gather.27.cloned.1.call-update) | async-done | bytes 8388624 | tf_op jit(solution)/shard_map/all_gather | solution.py:55
  421.4 27.5 %multiply_convert_fusion.1 = (bf16[256,4096]{1,0:T(8,128)(2,1)}, f32[256,4096]{1,0:T(8,128)}, f32[256,4096]{1,0:T(8,128)}) fusion(f32[4096]{0:T(1024)S(1)} %convert_element_type.233, bf16[256,1024]{1,0:T(8,128)(2,1)} %fusion.32, bf16[1024,4096]{1,0:T(8,128)(2,1)} %all-gather.27.cloned.1.call-done), kind=kOutput, calls=%fused_computation.18 | convolution fusion | flops 2216689664 | bytes 19415040 | tf_op jit(solution)/shard_map/dot_general | solution.py:26
  448.9 121.8 %all-gather.29.cloned.1.call-done = bf16[4096,1024]{1,0:T(8,128)(2,1)} async-done(((bf16[1024,1024]{1,0:T(8,128)(2,1)}), bf16[4096,1024]{1,0:T(8,128)(2,1)}) %all-gather.29.cloned.1.call-update) | async-done | bytes 8388624 | tf_op jit(solution)/shard_map/all_gather | solution.py:57
  570.7 6.5 fusion.44
  581.2 11.0 fusion.38
  592.2 6.9 multiply_reduce_fusion.1
  600.7 3.3 convolution_convert_fusion.6
  605.3 9.9 fusion.15
  615.3 13.0 %multiply_reduce_fusion = (f32[16,256]{1,0:T(8,128)S(1)}, f32[16,256,1024]{2,1,0:T(8,128)}) fusion(f32[16,256,1024]{2,1,0:T(8,128)} %copy-done, f32[16,256]{1,0:T(8,128)S(1)} %log_add_fusion, pred[256,1024]{1,0:T(8,128)(4,1)S(1)} %broadcast_compare_fusion, bf16[256,16,64]{0,2,1:T(8,128)(2,1)S(1)} %bitcast.91, bf16[1024,16,64]{0,2,1:T(8,128)(2,1)} %bitcast.86), kind=kOutput, calls=%fused_computation.1 | convolution fusion | flops 553644032 | bytes 36470784 | tf_op jit(solution)/shard_map/qhd,khd->hqk/dot_general | solution.py:145
  628.3 12.2 multiply_convert_fusion
  640.5 3.5 convolution_convert_fusion.2
  646.4 6.9 fusion.45
  653.3 4.1 reduce-scatter.5.cloned.1.call-done
  657.4 46.2 %reduce-scatter.3.cloned.1.call-done = bf16[256,1024]{0,1:T(8,128)(2,1)} async-done(((bf16[1024,1024]{0,1:T(8,128)(2,1)}), bf16[256,1024]{0,1:T(8,128)(2,1)}) %reduce-scatter.3.cloned.1.call-update) | async-done | bytes 524304 | tf_op jit(solution)/shard_map/reduce_scatter | solution.py:161
  707.4 3.5 all-to-all-start
  711.9 27.8 %all-to-all-done = bf16[256,4,256]{0,2,1:T(8,128)(2,1)S(1)} async-done(((bf16[256,4,256]{0,2,1:T(8,128)(2,1)}), bf16[256,4,256]{0,2,1:T(8,128)(2,1)S(1)}, u32[]{:S(2)}, u32[]{:S(2)}) %all-to-all-start) | async-done | bytes 524320 | tf_op jit(solution)/shard_map/all_to_all | solution.py:188
  739.7 3.5 all-to-all-start.1
  744.7 23.1 %all-to-all-done.1 = bf16[256,4,256]{2,0,1:T(8,128)(2,1)S(1)} async-done(((bf16[256,4,256]{2,0,1:T(8,128)(2,1)}), bf16[256,4,256]{2,0,1:T(8,128)(2,1)S(1)}, u32[]{:S(2)}, u32[]{:S(2)}) %all-to-all-start.1) | async-done | bytes 524320 | tf_op jit(solution)/shard_map/all_to_all | solution.py:189
  768.6 3.6 all-to-all-start.3
  774.1 77.8 %all-to-all-done.3 = bf16[256,4,1024]{2,0,1:T(8,128)(2,1)S(1)} async-done(((bf16[256,4,1024]{2,0,1:T(8,128)(2,1)}), bf16[256,4,1024]{2,0,1:T(8,128)(2,1)S(1)}, u32[]{:S(2)}, u32[]{:S(2)}) %all-to-all-start.3) | async-done | bytes 2097184 | tf_op jit(solution)/shard_map/all_to_all | solution.py:191
  851.8 3.5 all-to-all-start.2
  855.6 3.3 convolution_convert_fusion.5
  858.9 5.6 convolution_convert_fusion.3
  864.4 13.2 %all-to-all-done.2 = bf16[256,4,256]{2,0,1:T(8,128)(2,1)S(1)} async-done(((bf16[256,4,256]{2,0,1:T(8,128)(2,1)}), bf16[256,4,256]{2,0,1:T(8,128)(2,1)S(1)}, u32[]{:S(2)}, u32[]{:S(2)}) %all-to-all-start.2) | async-done | bytes 524320 | tf_op jit(solution)/shard_map/all_to_all | solution.py:190
  877.6 127.3 %all-gather.35.cloned.1.call-done = bf16[1024,4096]{1,0:T(8,128)(2,1)} async-done(((bf16[256,4096]{1,0:T(8,128)(2,1)}), bf16[1024,4096]{1,0:T(8,128)(2,1)}) %all-gather.35.cloned.1.call-update) | async-done | bytes 8388624 | tf_op jit(solution)/shard_map/all_gather | solution.py:184
  1004.9 7.1 convolution_convert_fusion
  1012.0 108.8 %all-gather.31.cloned.1.call-done = bf16[1024,3072]{0,1:T(8,128)(2,1)} async-done(((bf16[256,3072]{0,1:T(8,128)(2,1)}), bf16[1024,3072]{0,1:T(8,128)(2,1)}) %all-gather.31.cloned.1.call-update) | async-done | bytes 6291472 | tf_op jit(solution)/shard_map/all_gather | solution.py:182
  1120.8 5.7 fusion.14
  1129.9 16.2 %all-reduce.11 = (bf16[1024]{0:T(1024)(128)(2,1)S(1)}, bf16[1024]{0:T(1024)(128)(2,1)S(1)}, bf16[1024]{0:T(1024)(128)(2,1)S(1)}, bf16[1024]{0:T(1024)(128)(2,1)S...) all-reduce(bf16[1024]{0:T(1024)(128)(2,1)S(1)} %reduce_sum.234, ...), channel_id=4, replica_groups=mesh['replica'=8,'group'=4] {'group'}, use_global_device_ids=true, to_apply=%region_15.16.clone | all-reduce | flops 12288 | bytes 49152
  1146.7 13.0 %all-reduce.9 = (bf16[256]{0:T(256)(128)(2,1)S(1)}, bf16[256]{0:T(256)(128)(2,1)S(1)}, bf16[256]{0:T(256)(128)(2,1)S(1)}, bf16[256]{0:T(256)(128)(2,1)S(1)}, bf1...) all-reduce(bf16[256]{0:T(256)(128)(2,1)S(1)} %dynamic-slice.1, ...), channel_id=1, replica_groups=mesh['replica'=8,'group'=4] {'replica'}, use_global_device_ids=true, to_apply=%region_16.17 | all-reduce | flops 3072 | bytes 12288 | tf_op jit(solution)/shard_map/psum | solution.py:239
  1164.8 5.7 fusion.23
  1170.5 59.7 %all-reduce.14.cloned.1.call-done = (bf16[256,3072]{0,1:T(8,128)(2,1)}, bf16[256,1024]{1,0:T(8,128)(2,1)}, bf16[256,4096]{1,0:T(8,128)(2,1)}, bf16[1024,1024]{1,0:T(8,128)(2,1)}) async-done(((bf16[256,3072]{0,1:T(8,128)(2,1)}, bf16[256,1024]{1,0:T(8,128)(2,1)}, bf16[256,4096]{1,0:T(8,128)(2,1)}, bf16[1024,1024]{1,0:T(8,128)(2,1)}), (bf16[256,3072]{0,1:T(8,128)(2,1)}, bf16[256,1024]{1,0:T(8,128)(2,1)}, ...) | async-done | bytes 6291472 | tf_op jit(solution)/shard_map/psum | solution.py:238
  (174 shorter events, 54.1 us)
Async XLA Ops:
  7.2 120.5 %all-gather.19.cloned.1.call-start = ((), (), s32[]{:S(2)}) async-start(), calls=%async_computation.6 | async-start | bytes 7864320 | tf_op jit(solution)/shard_map/all_gather | solution.py:48
  7.9 192.2 %all-gather.21.cloned.1.call-start = ((), (), s32[]{:S(2)}) async-start(), calls=%async_computation.7 | async-start | bytes 2621440 | tf_op jit(solution)/shard_map/all_gather | solution.py:87
  133.7 2.8 copy-start.28
  133.7 10.9 copy-start.27
  133.7 22.8 %copy-start.29 = (bf16[256]{0:T(256)(128)(2,1)S(1)}, bf16[256]{0:T(256)(128)(2,1)}, u32[]{:S(2)}) copy-start(bf16[256]{0:T(256)(128)(2,1)} %param.21) | copy-start | bytes 1540
  133.7 31.3 %copy-start.30 = (bf16[256]{0:T(256)(128)(2,1)S(1)}, bf16[256]{0:T(256)(128)(2,1)}, u32[]{:S(2)}) copy-start(bf16[256]{0:T(256)(128)(2,1)} %param.23) | copy-start | bytes 1540
  133.7 40.3 %copy-start.31 = (bf16[256]{0:T(256)(128)(2,1)S(1)}, bf16[256]{0:T(256)(128)(2,1)}, u32[]{:S(2)}) copy-start(bf16[256]{0:T(256)(128)(2,1)} %param.22) | copy-start | bytes 1540
  133.7 48.5 %copy-start.32 = (bf16[256]{0:T(256)(128)(2,1)S(1)}, bf16[256]{0:T(256)(128)(2,1)}, u32[]{:S(2)}) copy-start(bf16[256]{0:T(256)(128)(2,1)} %param.28) | copy-start | bytes 1540
  133.7 57.6 %copy-start.33 = (bf16[256]{0:T(256)(128)(2,1)S(1)}, bf16[256]{0:T(256)(128)(2,1)}, u32[]{:S(2)}) copy-start(bf16[256]{0:T(256)(128)(2,1)} %param.29) | copy-start | bytes 1540
  133.7 65.9 %copy-start.26 = (s32[1024]{0:T(1024)S(1)}, s32[1024]{0:T(1024)}, u32[]{:S(2)}) copy-start(s32[1024]{0:T(1024)} %param.30) | copy-start | bytes 12292
  133.7 91.6 %all-gather.23.cloned.1.call-start = ((), (), s32[]{:S(2)}) async-start(), calls=%async_computation.8 | async-start | bytes 2621440 | tf_op jit(solution)/shard_map/all_gather | solution.py:86
  134.7 65.2 %copy-start.21 = (bf16[256,1024]{1,0:T(8,128)(2,1)S(1)}, bf16[256,1024]{1,0:T(8,128)(2,1)}, u32[]{:S(2)}) copy-start(bf16[256,1024]{1,0:T(8,128)(2,1)} %get-tuple-element.114) | copy-start | bytes 1572868
  134.7 136.7 %all-gather.25.cloned.1.call-start = ((), (), s32[]{:S(2)}) async-start(), calls=%async_computation.9 | async-start | bytes 2621440 | tf_op jit(solution)/shard_map/all_gather | solution.py:51
  135.3 286.2 %all-gather.27.cloned.1.call-start = ((), (), s32[]{:S(2)}) async-start(), calls=%async_computation.10 | async-start | bytes 10485760 | tf_op jit(solution)/shard_map/all_gather | solution.py:55
  135.9 434.9 %all-gather.29.cloned.1.call-start = ((), (), s32[]{:S(2)}) async-start(), calls=%async_computation.11 | async-start | bytes 10485760 | tf_op jit(solution)/shard_map/all_gather | solution.py:57
  136.4 521.0 %reduce-scatter.5.cloned.1.call-start = ((), (), s32[]{:S(2)}) async-start(), calls=%async_computation.13 | async-start | bytes 2621440 | tf_op jit(solution)/shard_map/reduce_scatter | solution.py:167
  200.1 28.1 %copy-start.3 = (bf16[256,1024]{0,1:T(8,128)(2,1)}, bf16[256,1024]{0,1:T(8,128)(2,1)S(1)}, u32[]{:S(2)}) copy-start(bf16[256,1024]{0,1:T(8,128)(2,1)S(1)} %copy.59) | copy-start | bytes 1572868
  230.8 6.5 copy-start
  230.8 6.5 copy-start.2
  570.7 6.8 copy-start.5
  600.7 14.5 %copy-start.17 = (bf16[256,1024]{1,0:T(8,128)(2,1)}, bf16[256,1024]{1,0:T(8,128)(2,1)S(1)}, u32[]{:S(2)}) copy-start(bf16[256,1024]{1,0:T(8,128)(2,1)S(1)} %get-tuple-element.107) | copy-start | bytes 1572868
  615.2 88.4 %reduce-scatter.3.cloned.1.call-start = ((), (), s32[]{:S(2)}) async-start(), calls=%async_computation.12 | async-start | bytes 2621440 | tf_op jit(solution)/shard_map/reduce_scatter | solution.py:161
  628.3 12.2 copy-start.4
  640.4 3.9 copy-start.1
  644.3 211.2 %all-gather.33.cloned.1.call-start = ((), (), s32[]{:S(2)}) async-start(), calls=%async_computation.15 | async-start | bytes 2621440 | tf_op jit(solution)/shard_map/all_gather | solution.py:183
  645.1 213.8 %all-gather.37.cloned.1.call-start = ((), (), s32[]{:S(2)}) async-start(), calls=%async_computation.17 | async-start | bytes 2621440 | tf_op jit(solution)/shard_map/all_gather | solution.py:185
  645.7 359.2 %all-gather.35.cloned.1.call-start = ((), (), s32[]{:S(2)}) async-start(), calls=%async_computation.16 | async-start | bytes 10485760 | tf_op jit(solution)/shard_map/all_gather | solution.py:184
  646.4 474.4 %all-gather.31.cloned.1.call-start = ((), (), s32[]{:S(2)}) async-start(), calls=%async_computation.14 | async-start | bytes 7864320 | tf_op jit(solution)/shard_map/all_gather | solution.py:182
  653.3 53.1 %copy-start.12 = (bf16[256,1024]{1,0:T(8,128)(2,1)S(1)}, bf16[256,1024]{1,0:T(8,128)(2,1)}, u32[]{:S(2)}) copy-start(bf16[256,1024]{1,0:T(8,128)(2,1)} %param.16) | copy-start | bytes 1572868
  653.3 57.5 %copy-start.13 = (bf16[16,64,256]{2,1,0:T(8,128)(2,1)S(1)}, bf16[16,64,256]{2,1,0:T(8,128)(2,1)}, u32[]{:S(2)}) copy-start(bf16[16,64,256]{2,1,0:T(8,128)(2,1)} %fusion.24) | copy-start | bytes 1572868
  703.6 39.5 %copy-start.14 = (bf16[256,4096]{1,0:T(8,128)(2,1)S(1)}, bf16[256,4096]{1,0:T(8,128)(2,1)}, u32[]{:S(2)}) copy-start(bf16[256,4096]{1,0:T(8,128)(2,1)} %get-tuple-element.112) | copy-start | bytes 6291460
  707.4 32.3 %all-to-all-start = ((bf16[256,4,256]{0,2,1:T(8,128)(2,1)}), bf16[256,4,256]{0,2,1:T(8,128)(2,1)S(1)}, u32[]{:S(2)}, u32[]{:S(2)}) async-start(bf16[256,4,256]{0,2,1:T(8,128)(2,1)} %bitcast.101), calls=%async_computation.2 | async-start | bytes 1048576 | tf_op jit(solution)/shard_map/all_to_all | solution.py:188
  739.7 3.5 copy-start.18
  739.7 28.2 %all-to-all-start.1 = ((bf16[256,4,256]{2,0,1:T(8,128)(2,1)}), bf16[256,4,256]{2,0,1:T(8,128)(2,1)S(1)}, u32[]{:S(2)}, u32[]{:S(2)}) async-start(bf16[256,4,256]{2,0,1:T(8,128)(2,1)} %copy.64), calls=%async_computation.3 | async-start | bytes 1048576 | tf_op jit(solution)/shard_map/all_to_all | solution.py:189
  743.2 30.1 %copy-start.16 = (bf16[256,1024]{1,0:T(8,128)(2,1)S(1)}, bf16[256,1024]{1,0:T(8,128)(2,1)}, u32[]{:S(2)}) copy-start(bf16[256,1024]{1,0:T(8,128)(2,1)} %fusion.32) | copy-start | bytes 1572868
  744.7 27.5 %copy-start.19 = (bf16[256,4,256]{0,2,1:T(8,128)(2,1)S(1)}, bf16[256,4,256]{0,2,1:T(8,128)(2,1)}, u32[]{:S(2)}) copy-start(bf16[256,4,256]{0,2,1:T(8,128)(2,1)} %copy-done.18) | copy-start | bytes 1572868
  768.6 83.2 %all-to-all-start.3 = ((bf16[256,4,1024]{2,0,1:T(8,128)(2,1)}), bf16[256,4,1024]{2,0,1:T(8,128)(2,1)S(1)}, u32[]{:S(2)}, u32[]{:S(2)}) async-start(bf16[256,4,1024]{2,0,1:T(8,128)(2,1)} %bitcast.80), calls=%async_computation.5 | async-start | bytes 4194304 | tf_op jit(solution)/shard_map/all_to_all | solution.py:191
  851.8 25.8 %all-to-all-start.2 = ((bf16[256,4,256]{2,0,1:T(8,128)(2,1)}), bf16[256,4,256]{2,0,1:T(8,128)(2,1)S(1)}, u32[]{:S(2)}, u32[]{:S(2)}) async-start(bf16[256,4,256]{2,0,1:T(8,128)(2,1)} %bitcast.81), calls=%async_computation.4 | async-start | bytes 1048576 | tf_op jit(solution)/shard_map/all_to_all | solution.py:190
  855.3 374.9 %all-reduce.14.cloned.1.call-start = ((), (), s32[]{:S(2)}) async-start(), calls=%async_computation.18 | async-start | bytes 12582912 | tf_op jit(solution)/shard_map/psum | solution.py:238
  1004.9 115.9 %copy-start.24 = (bf16[4,256,256]{2,1,0:T(8,128)(2,1)S(1)}, bf16[4,256,256]{2,1,0:T(8,128)(2,1)}, u32[]{:S(2)}) copy-start(bf16[4,256,256]{2,1,0:T(8,128)(2,1)} %copy.63) | copy-start | bytes 1572868
  1126.5 1.1 copy-start.34
  1126.5 3.1 copy-start.20
  1126.5 38.3 %copy-start.8 = (f32[256,1024]{1,0:T(8,128)S(1)}, f32[256,1024]{1,0:T(8,128)}, u32[]{:S(2)}) copy-start(f32[256,1024]{1,0:T(8,128)} %copy-done.7) | copy-start | bytes 3145732
  1126.5 38.3 %copy-start.15 = (bf16[16,64,256]{2,1,0:T(8,128)(2,1)S(1)}, bf16[16,64,256]{2,1,0:T(8,128)(2,1)}, u32[]{:S(2)}) copy-start(bf16[16,64,256]{2,1,0:T(8,128)(2,1)} %get-tuple-element.128) | copy-start | bytes 1572868
  1126.6 38.3 %copy-start.25 = (bf16[256,1024]{0,1:T(8,128)(2,1)S(1)}, bf16[256,1024]{0,1:T(8,128)(2,1)}, u32[]{:S(2)}) copy-start(bf16[256,1024]{0,1:T(8,128)(2,1)} %reduce-scatter.3.cloned.1.call-done) | copy-start | bytes 1572868
  1230.2 3.2 copy-start.23
  1230.2 4.3 copy-start.11
  1233.4 3.6 copy-start.10
  (4 other events, 3.8 us)
Sparse Core Ops, SparseCore 0:
  9.6 118.0 all-gather.18
  133.9 44.5 all-gather.20
  180.6 44.7 all-gather.22
  226.8 44.6 all-gather.24
  272.8 148.5 all-gather.26
  422.8 147.8 all-gather.28
  615.3 42.0 reduce-scatter.4
  660.4 43.1 reduce-scatter.2
  705.2 65.6 all-gather.32
  772.3 75.8 all-gather.36
  849.8 155.0 all-gather.34
  1006.9 113.8 all-gather.30
  1126.7 103.4 all-reduce.13
where the time goes:
time: 1250 us
  waiting for transfers between devices  908 us (73%)
  matrix products  131 us (10%)
  blocking collectives  113 us (9%)
  other arithmetic  36.7 us (3%)
  local copies, waits for them, and re-layouts  27.3 us (2%)
  between operations  15.9 us (1%)
  starting transfers between devices  14.7 us (1%)
    all_gather x1, waiting for transfers between devices, on_device(): lax.all_gather(inner_weight, 'group', axis=0, tiled=True)  146 us
    all_gather x1, waiting for transfers between devices, on_device(): lax.all_gather(inner_grad, 'group', axis=0, tiled=True)  127 us
    all_gather x1, waiting for transfers between devices, on_device(): lax.all_gather(outer_weight, 'group', axis=0, tiled=True)  122 us
    all_gather x1, waiting for transfers between devices, on_device(): lax.all_gather(projected_grad, 'group', axis=0, tiled=True)  109 us
    all_gather x1, waiting for transfers between devices, on_device(): lax.all_gather(qkv_weight, 'group', axis=0, tiled=True)  97.9 us
    dot_general x12, matrix products, matmul(): return jnp.dot(left, right, preferred_element_type=jnp.float32)  90 us
    all_to_all x1, waiting for transfers between devices, on_device(): lax.all_to_all(activated, 'group', split_axis=1, concat_axis=0, tiled=True)  77.8 us
    psum x1, waiting for transfers between devices, on_device(): lax.psum(owned[0].astype(jnp.bfloat16), 'replica').astype(jnp.float32)  59.7 us
  transfers between devices with their start and end apart: 17, of which 14 were waited for; matrix products, arithmetic and copies ran while one was open for 10% of the time, Pallas kernels for 0%

commit v1 on v0

v1 whole, which is shorter than its diff:
```python
import jax
import jax.numpy as jnp
from jax import lax
from jax.sharding import PartitionSpec as P

D = 1024
HEADS = 16
HD = 64


NORM_EPS = 1e-05


def layer_norm(resid, gain, shift):
    average = jnp.mean(resid, axis=-1, keepdims=True)
    centred = resid - average
    variance = jnp.mean(centred * centred, axis=-1, keepdims=True)
    return centred * lax.rsqrt(variance + NORM_EPS) * gain + shift


def gelu_exact(values):
    return jax.nn.gelu(values, approximate=False)


def matmul(left, right):
    return jnp.dot(left, right, preferred_element_type=jnp.float32)


def on_device(
    layer_input,
    qkv_weight,
    query_bias,
    value_bias,
    attn_weight,
    attn_bias,
    first_gain,
    first_shift,
    inner_weight,
    inner_bias,
    outer_weight,
    outer_bias,
    second_gain,
    second_shift,
    segment_ids,
    output_grad,
):
    groups, replicas = lax.axis_size("group"), lax.axis_size("replica")
    group_place, replica_place = lax.axis_index("group"), lax.axis_index("replica")
    row_count = layer_input.shape[0]
    length = segment_ids.shape[0]
    own = query_bias.shape[0]
    hidden = inner_bias.shape[0]
    heads = own // HD
    piece = own // replicas
    score_scale = HD ** (-0.5)

    qkv_rows = lax.dynamic_slice_in_dim(qkv_weight, replica_place * piece, piece)
    inner_rows = lax.dynamic_slice_in_dim(inner_weight, replica_place * piece, piece)
    qkv_rows = qkv_rows.reshape(piece, 3, groups, own).transpose(2, 0, 1, 3)
    inner_rows = inner_rows.reshape(piece, groups, hidden).transpose(1, 0, 2)
    moved = jnp.concatenate([qkv_rows.reshape(groups, piece, 3 * own), inner_rows], axis=2)
    moved = lax.all_to_all(moved, "group", split_axis=0, concat_axis=0, tiled=True)

    def spread(shares):
        every = lax.all_gather(shares, "replica", axis=0)
        return every.transpose(1, 0, 2, 3).reshape(D, shares.shape[-1])

    qkv_cols = spread(moved[:, :, : 3 * own])
    input_all = lax.all_gather(layer_input, "group", axis=0, tiled=True)
    inner_cols = spread(moved[:, :, 3 * own :])
    vectors = jnp.stack(
        [attn_bias, first_gain, first_shift, outer_bias, second_gain, second_shift]
    )
    vectors = lax.all_gather(vectors, "group", axis=0).transpose(1, 0, 2).reshape(6, D)
    attn_bias_full, gain_one, shift_one, outer_bias_full, gain_two, shift_two = vectors

    projected = matmul(input_all, qkv_cols)
    queries = ((projected[:, :own] + query_bias) * score_scale).astype(jnp.bfloat16)
    key_rows = projected[:, own : 2 * own].astype(jnp.bfloat16)
    value_rows = (projected[:, 2 * own :] + value_bias).astype(jnp.bfloat16)
    allowed = segment_ids[:, None] == segment_ids[None, :]
    query_heads = queries.reshape(length, heads, HD)
    key_heads = key_rows.reshape(length, heads, HD)
    value_heads = value_rows.reshape(length, heads, HD)

    def masked_scores():
        raw = jnp.einsum("qhd,khd->hqk", query_heads, key_heads, preferred_element_type=jnp.float32)
        return jnp.where(allowed[None], raw, -1e30)

    scores = masked_scores()
    row_peak = jnp.max(scores, axis=-1, keepdims=True)
    exponent = jnp.exp(scores - row_peak)
    row_total = jnp.sum(exponent, axis=-1, keepdims=True)
    log_total = row_peak + jnp.log(row_total)
    attn_probs = (exponent / row_total).astype(jnp.bfloat16)
    attended = jnp.einsum(
        "hqk,khd->qhd", attn_probs, value_heads, preferred_element_type=jnp.float32
    )
    attended = attended.reshape(length, own).astype(jnp.bfloat16)

    def to_owner(terms):
        return lax.psum_scatter(
            terms.astype(jnp.bfloat16), "group", scatter_dimension=0, tiled=True
        ).astype(jnp.float32)

    def to_all(rows):
        return lax.all_gather(rows, "group", axis=0, tiled=True)

    branch = to_owner(matmul(attended, attn_weight)) + attn_bias_full
    residual_one = layer_input.astype(jnp.float32) + branch
    first, first_pull = jax.vjp(
        layer_norm, residual_one, gain_one.astype(jnp.float32), shift_one.astype(jnp.float32)
    )
    first_all = to_all(first.astype(jnp.bfloat16))
    inner = matmul(first_all, inner_cols) + inner_bias
    activated_f, gelu_pull = jax.vjp(gelu_exact, inner)
    activated = activated_f.astype(jnp.bfloat16)
    outer = to_owner(matmul(activated, outer_weight)) + outer_bias_full
    result, second_pull = jax.vjp(
        layer_norm, first + outer, gain_two.astype(jnp.float32), shift_two.astype(jnp.float32)
    )
    layer_output = result.astype(jnp.bfloat16)
    second_res_grad, second_gain_grad, second_shift_grad = second_pull(
        output_grad.astype(jnp.float32)
    )
    outer_grad = second_res_grad.astype(jnp.bfloat16)
    outer_bias_grad = jnp.sum(outer_grad.astype(jnp.float32), axis=0)
    outer_all = to_all(outer_grad)
    inner_grad = gelu_pull(matmul(outer_all, outer_weight.T))[0].astype(jnp.bfloat16)
    inner_bias_grad = jnp.sum(inner_grad.astype(jnp.float32), axis=0)
    first_grad = second_res_grad + to_owner(matmul(inner_grad, inner_cols.T))
    outer_weight_grad = matmul(activated.T, outer_all).astype(jnp.bfloat16)
    outer_weight_grad = lax.psum(outer_weight_grad, "replica").astype(jnp.float32)

    def to_rows(columns):
        width = columns.shape[-1]
        parts = columns.astype(jnp.bfloat16).reshape(groups, replicas, piece, width)
        parts = parts.transpose(1, 0, 2, 3)
        summed = lax.psum_scatter(parts, "replica", scatter_dimension=0)
        summed = lax.all_to_all(summed, "group", split_axis=0, concat_axis=0, tiled=True)
        return lax.all_gather(summed, "replica", axis=0)

    inner_weight_grad = to_rows(matmul(first_all.T, inner_grad))
    inner_weight_grad = inner_weight_grad.transpose(0, 2, 1, 3).reshape(own, groups * hidden)
    inner_weight_grad = inner_weight_grad.astype(jnp.float32)

    first_res_grad, first_gain_grad, first_shift_grad = first_pull(first_grad)
    branch_grad = first_res_grad.astype(jnp.bfloat16)
    attn_bias_grad = jnp.sum(branch_grad.astype(jnp.float32), axis=0)
    branch_all = to_all(branch_grad)
    attended_grad = matmul(branch_all, attn_weight.T).astype(jnp.bfloat16)
    attended_grad = attended_grad.reshape(length, heads, HD)
    attn_weight_grad = matmul(attended.T, branch_all).astype(jnp.bfloat16)
    attn_weight_grad = lax.psum(attn_weight_grad, "replica").astype(jnp.float32)

    probs = jnp.exp(masked_scores() - log_total)
    probs_low = probs.astype(jnp.bfloat16)
    probs_grad = jnp.einsum(
        "qhd,khd->hqk", attended_grad, value_heads, preferred_element_type=jnp.float32
    )
    values_grad = jnp.einsum(
        "hqk,qhd->khd", probs_low, attended_grad, preferred_element_type=jnp.float32
    )
    weighted = jnp.sum(probs * probs_grad, axis=-1, keepdims=True)
    scores_grad = (probs * (probs_grad - weighted)).astype(jnp.bfloat16)
    queries_grad = jnp.einsum(
        "hqk,khd->qhd", scores_grad, key_heads, preferred_element_type=jnp.float32
    )
    keys_grad = jnp.einsum(
        "hqk,qhd->khd", scores_grad, query_heads, preferred_element_type=jnp.float32
    )
    queries_grad = queries_grad.reshape(length, own).astype(jnp.bfloat16)
    scaled_queries = (queries_grad.astype(jnp.float32) * score_scale).astype(jnp.bfloat16)
    keys_grad = keys_grad.reshape(length, own).astype(jnp.bfloat16)
    values_grad = values_grad.reshape(length, own).astype(jnp.bfloat16)
    projected_grad = jnp.concatenate([scaled_queries, keys_grad, values_grad], axis=1)
    input_terms = to_owner(matmul(projected_grad, qkv_cols.T))
    input_grad = (first_res_grad + input_terms).astype(jnp.bfloat16)
    qkv_weight_grad = to_rows(matmul(input_all.T, projected_grad))
    qkv_weight_grad = qkv_weight_grad.reshape(replicas, groups, piece, 3, own)
    qkv_weight_grad = qkv_weight_grad.transpose(0, 2, 3, 1, 4).reshape(own, 3 * D)
    qkv_weight_grad = qkv_weight_grad.astype(jnp.float32)

    query_bias_grad = jnp.sum(scaled_queries.astype(jnp.float32), axis=0)
    value_bias_grad = jnp.sum(values_grad.astype(jnp.float32), axis=0)
    shared = jnp.stack(
        [
            attn_bias_grad,
            first_gain_grad,
            first_shift_grad,
            outer_bias_grad,
            second_gain_grad,
            second_shift_grad,
        ]
    )
    shared = shared.reshape(6, groups, own).transpose(1, 0, 2).reshape(groups, 6 * own)
    mine = jnp.concatenate([query_bias_grad, value_bias_grad, inner_bias_grad])
    is_mine = jnp.arange(groups)[:, None] == group_place
    terms = jnp.concatenate([shared, jnp.where(is_mine, mine[None], 0.0)], axis=1)
    terms = lax.psum(terms, ("replica", "group"))
    terms = lax.dynamic_index_in_dim(terms, group_place, keepdims=False)
    small = terms[: 8 * own].reshape(8, own)
    return (
        layer_output,
        input_grad,
        qkv_weight_grad,
        small[6],
        small[7],
        attn_weight_grad,
        small[0],
        small[1],
        small[2],
        inner_weight_grad,
        terms[8 * own :],
        outer_weight_grad,
        small[3],
        small[4],
        small[5],
    )


def solution(mesh):
    in_specs = (
        P(("replica", "group"), None),
        P("group", None),
        P("group"),
        P("group"),
        P("group", None),
        P("group"),
        P("group"),
        P("group"),
        P("group", None),
        P("group"),
        P("group", None),
        P("group"),
        P("group"),
        P("group"),
        P("replica"),
        P(("replica", "group"), None),
    )
    out_specs = (
        P(("replica", "group"), None),
        P(("replica", "group"), None),
        P("group", None),
        P("group"),
        P("group"),
        P("group", None),
        P("group"),
        P("group"),
        P("group"),
        P("group", None),
        P("group"),
        P("group", None),
        P("group"),
        P("group"),
        P("group"),
    )
    return jax.shard_map(
        on_device, mesh=mesh, in_specs=in_specs, out_specs=out_specs, check_vma=False
    )
```

time: 1250 us -> 762 us (0.61)
  waiting for transfers between devices: 908 us -> 438 us
  matrix products: 131 us -> 95.5 us
  local copies, waits for them, and re-layouts: 27.3 us -> 50.1 us
  starting transfers between devices: 14.7 us -> 1.15 us
    all_gather x10 -> x8, waiting for transfers between devices: 652 us -> 225 us  [the longest x3 125 us: to_all(): return lax.all_gather(rows, 'group', axis=0, tiled=True)]
    all_to_all x4 -> x0, waiting for transfers between devices: 142 us -> none  [the longest x1 77.8 us: on_device(): lax.all_to_all(activated, 'group', split_axis=1, concat_axis=0, tiled=True)]
    unnamed x13 -> x14, waiting for transfers between devices: 4.26 us -> 99.7 us
    all_gather x9 -> x1, blocking collectives: 83.4 us -> 13.6 us  [on_device(): lax.all_gather(vectors, 'group', axis=0).transpose(1, 0, 2).reshape(6, D)]
    reduce_scatter x2 -> x4, waiting for transfers between devices: 50.3 us -> 113 us  [to_owner(): lax.psum_scatter(terms.astype(jnp.bfloat16), 'group', scatter_dimension=0...]
    psum x1 -> x0, waiting for transfers between devices: 59.7 us -> none  [on_device(): lax.psum(owned[0].astype(jnp.bfloat16), 'replica').astype(jnp.float32)]
    all_to_all x0 -> x3, blocking collectives: none -> 53 us  [the longest x2 33.8 us: to_rows(): lax.all_to_all(summed, 'group', split_axis=0, concat_axis=0, tiled=True)]
    dot_general x12, matrix products: 90 us -> 55.4 us  [matmul(): return jnp.dot(left, right, preferred_element_type=jnp.float32)]
  transfers between devices with their start and end apart: 17 -> 13, of which waited for: 14 -> 11; matrix products, arithmetic and copies ran while one was open for 10% -> 8% of each run, Pallas kernels for 0% -> 0%
where the time goes in v1:
time: 762 us; the launch traced here: 753 us
  waiting for transfers between devices  438 us (57%)
  blocking collectives  104 us (14%)
  matrix products  95.5 us (13%)
  local copies, waits for them, and re-layouts  50.1 us (7%)
  other arithmetic  48.7 us (6%)
  between operations  15 us (2%)
    all_gather x3, waiting for transfers between devices, to_all(): return lax.all_gather(rows, 'group', axis=0, tiled=True)  125 us
    reduce_scatter x4, waiting for transfers between devices, to_owner(): lax.psum_scatter(terms.astype(jnp.bfloat16), 'group', scatter_dimension=0...  113 us
    unnamed x14, waiting for transfers between devices  99.7 us
    dot_general x12, matrix products, matmul(): return jnp.dot(left, right, preferred_element_type=jnp.float32)  55.4 us
    all_gather x2, waiting for transfers between devices, spread(): every = lax.all_gather(shares, 'replica', axis=0)  47.8 us
    all_gather x1, waiting for transfers between devices, on_device(): input_all = lax.all_gather(layer_input, 'group', axis=0, tiled=True)  44.9 us
    psum x1, blocking collectives, on_device(): terms = lax.psum(terms, ('replica', 'group'))  37.7 us
    all_to_all x2, blocking collectives, to_rows(): lax.all_to_all(summed, 'group', split_axis=0, concat_axis=0, tiled=True)  33.8 us
  transfers between devices with their start and end apart: 13, of which 11 were waited for; matrix products, arithmetic and copies ran while one was open for 8% of the time, Pallas kernels for 0%

profile of v1, /device:TPU:0, one launch (start us, length us, event | category | flops | bytes accessed | tf_op | source)
XLA Modules:
  0.0 752.6 jit_solution(7292547148881540925)
XLA Ops:
  9.9 19.2 %all_to_all.15 = bf16[4,32,1792]{2,1,0:T(8,128)(2,1)S(1)} all-to-all(bf16[4,32,1792]{2,1,0:T(8,128)(2,1)S(1)} %copy.70), channel_id=1, replica_groups=mesh['replica'=8,'group'=4] {'group'}, dimensions={0} | all-to-all | bytes 917504 | tf_op jit(solution)/shard_map/all_to_all | solution.py:62
  32.1 23.4 %all-gather.23.cloned.1.call-done = bf16[32,32,768]{2,1,0:T(8,128)(2,1)} async-done(((bf16[4,32,768]{2,1,0:T(8,128)(2,1)}), bf16[32,32,768]{2,1,0:T(8,128)(2,1)}) %all-gather.23.cloned.1.call-update) | async-done | bytes 1572880 | tf_op jit(solution)/shard_map/all_gather | solution.py:65
  55.6 2.7 copy.71
  58.2 44.9 %all-gather.15.cloned.1.call-done = bf16[1024,1024]{1,0:T(8,128)(2,1)} async-done(((bf16[256,1024]{1,0:T(8,128)(2,1)}), bf16[1024,1024]{1,0:T(8,128)(2,1)}) %all-gather.15.cloned.1.call-update) | async-done | bytes 2097168 | tf_op jit(solution)/shard_map/all_gather | solution.py:69
  103.1 3.9 convolution_bitcast_fusion
  108.1 7.3 select_reduce_fusion
  115.4 8.8 %fusion = f32[4,1024]{1,0:T(4,128)S(1)} fusion(f32[4,1024,1024]{1,2,0:T(8,128)} %get-tuple-element.57, f32[4,1024]{1,0:T(4,128)S(1)} %get-tuple-element.56, pred[1024,1024]{0,1:T(8,128)(4,1)S(1)} %broadcast_compare_fusion), kind=kLoop, calls=%fused_computation.5 | loop fusion | flops 12578816 | bytes 17858560 | tf_op jit(solution)/shard_map/reduce_sum | solution.py:93
  124.2 8.2 %fusion.19 = bf16[4,64,1024]{2,1,0:T(8,128)(2,1)S(1)} fusion(bf16[1024,4,64]{0,2,1:T(8,128)(2,1)} %bitcast.124, f32[4,1024,1024]{1,2,0:T(8,128)} %get-tuple-element.57, f32[4,1024]{1,0:T(4,128)S(1)} %fusion, f32[4,1024]{1,0:T(4,128)S(1)} %get-tuple-element.56, pred[1024,1024]{0,1:T(8,128)(4,1)S(1)} %broadcast_compare_fusion), kind=kOutput, calls=%fused_computation.54 | convolution fusion | flops 553910272 | bytes 18907136 | tf_op jit(solution)/shard_map/hqk,khd->qhd/dot_general | solution.py:96
  133.2 2.1 convolution_convert_fusion.4
  137.3 13.6 %all-gather.5 = bf16[4,6,256]{2,1,0:T(8,128)(2,1)S(1)} all-gather(bf16[1,6,256]{2,1,0:T(8,128)(2,1)S(1)} %bitcast.162), channel_id=3, replica_groups=mesh['replica'=8,'group'=4] {'group'}, dimensions={0}, use_global_device_ids=true | all-gather | bytes 15360 | tf_op jit(solution)/shard_map/all_gather | solution.py:74
  150.9 27.3 %reduce-scatter.11.cloned.1.call-done = bf16[256,1024]{1,0:T(8,128)(2,1)} async-done(((bf16[1024,1024]{1,0:T(8,128)(2,1)}), bf16[256,1024]{1,0:T(8,128)(2,1)}) %reduce-scatter.11.cloned.1.call-update) | async-done | bytes 524304 | tf_op jit(solution)/shard_map/reduce_scatter | solution.py:102
  181.2 2.3 fusion.29
  183.6 24.3 %all-gather.25.cloned.1.call-done = bf16[32,32,1024]{2,1,0:T(8,128)(2,1)} async-done(((bf16[4,32,1024]{2,1,0:T(8,128)(2,1)}), bf16[32,32,1024]{2,1,0:T(8,128)(2,1)}) %all-gather.25.cloned.1.call-update) | async-done | bytes 2097168 | tf_op jit(solution)/shard_map/all_gather | solution.py:65
  208.0 3.2 copy.73
  211.2 44.9 %all-gather.17.cloned.1.call-done = bf16[1024,1024]{1,0:T(8,128)(2,1)} async-done(((bf16[256,1024]{1,0:T(8,128)(2,1)}), bf16[1024,1024]{1,0:T(8,128)(2,1)}) %all-gather.17.cloned.1.call-update) | async-done | bytes 2097168 | tf_op jit(solution)/shard_map/all_gather | solution.py:107
  256.0 14.7 %multiply_convert_fusion.1 = (bf16[1024,1024]{1,0:T(8,128)(2,1)S(1)}, f32[1024,1024]{1,0:T(8,128)}, f32[1024,1024]{1,0:T(8,128)}) fusion(f32[1024]{0:T(1024)S(1)} %convert_element_type.265, bf16[1024,1024]{1,0:T(8,128)(2,1)} %all-gather.17.cloned.1.call-done, bf16[1024,1024]{1,0:T(8,128)(2,1)} %bitcast.128), kind=kOutput, calls=%fused_computation.16 | convolution fusion | flops 2216689664 | bytes 14684160 | tf_op jit(solution)/shard_map/dot_general | solution.py:26
  272.0 3.7 convolution_convert_fusion.3
  275.8 42.7 %reduce-scatter.13.cloned.1.call-done = bf16[256,1024]{1,0:T(8,128)(2,1)} async-done(((bf16[1024,1024]{1,0:T(8,128)(2,1)}), bf16[256,1024]{1,0:T(8,128)(2,1)}) %reduce-scatter.13.cloned.1.call-update) | async-done | bytes 524304 | tf_op jit(solution)/shard_map/reduce_scatter | solution.py:102
  318.5 2.0 fusion.39
  325.9 45.0 %all-gather.19.cloned.1.call-done = bf16[1024,1024]{1,0:T(8,128)(2,1)} async-done(((bf16[256,1024]{1,0:T(8,128)(2,1)}), bf16[1024,1024]{1,0:T(8,128)(2,1)}) %all-gather.19.cloned.1.call-update) | async-done | bytes 2097168 | tf_op jit(solution)/shard_map/all_gather | solution.py:107
  370.9 7.0 convert_reduce_fusion
  379.2 3.7 convolution_convert_fusion.2
  383.0 42.7 %reduce-scatter.15.cloned.1.call-done = bf16[256,1024]{1,0:T(8,128)(2,1)} async-done(((bf16[1024,1024]{1,0:T(8,128)(2,1)}), bf16[256,1024]{1,0:T(8,128)(2,1)}) %reduce-scatter.15.cloned.1.call-update) | async-done | bytes 524304 | tf_op jit(solution)/shard_map/reduce_scatter | solution.py:102
  431.2 6.1 convolution_convert_fusion
  437.3 3.8 convolution_convert_fusion.1
  441.0 35.5 %all-gather.21.cloned.1.call-done = bf16[1024,1024]{1,0:T(8,128)(2,1)} async-done(((bf16[256,1024]{1,0:T(8,128)(2,1)}), bf16[1024,1024]{1,0:T(8,128)(2,1)}) %all-gather.21.cloned.1.call-update) | async-done | bytes 2097168 | tf_op jit(solution)/shard_map/all_gather | solution.py:107
  476.5 2.3 convolution_convert_fusion.10
  478.8 8.2 %convert_reduce_fusion.2 = (f32[4,64]{1,0:T(4,128)S(1)}, bf16[4,64,1024]{2,1,0:T(8,128)(2,1)S(1)}) fusion(bf16[1024,4,64]{0,2,1:T(8,128)(2,1)S(1)} %bitcast.136, f32[4,1024,1024]{1,2,0:T(8,128)} %get-tuple-element.57, f32[4,1024]{1,0:T(4,128)S(1)} %log_add_fusion, pred[1024,1024]{0,1:T(8,128)(4,1)S(1)} %broadcast_compare_fusion), kind=kOutput, calls=%fused_computation.65 | convolution fusion | flops 550240000 | bytes 18891776 | tf_op jit(solution)/shard_map/hqk,qhd->khd/dot_general | solution.py:161
  487.0 12.0 %multiply_reduce_fusion = (f32[4,1024]{1,0:T(4,128)S(1)}, f32[4,1024,1024]{1,2,0:T(8,128)}) fusion(f32[4,1024,1024]{1,2,0:T(8,128)} %get-tuple-element.57, f32[4,1024]{1,0:T(4,128)S(1)} %log_add_fusion, pred[1024,1024]{0,1:T(8,128)(4,1)S(1)} %broadcast_compare_fusion, bf16[1024,4,64]{0,2,1:T(8,128)(2,1)S(1)} %bitcast.137, bf16[1024,4,64]{0,2,1:T(8,128)(2,1)S(1)} %bitcast.125), kind=kOutput, calls=%fused_computation.1 | convolution fusion | flops 553644032 | bytes 35684352 | tf_op jit(solution)/shard_map/qhd,khd->hqk/dot_general | solution.py:158
  499.1 12.0 %multiply_convert_fusion = bf16[4,1024,1024]{1,2,0:T(8,128)(2,1)S(1)} fusion(f32[4,1024,1024]{1,2,0:T(8,128)} %get-tuple-element.60, f32[4,1024,1024]{1,2,0:T(8,128)} %get-tuple-element.57, f32[4,1024]{1,0:T(4,128)S(1)} %get-tuple-element.59, f32[4,1024]{1,0:T(4,128)S(1)} %log_add_fusion, pred[1024,1024]{0,1:T(8,128)(4,1)S(1)} %broadcast_compare_fusion), kind=kLoop, calls=%fused_computation | loop fusion | flops 20971520 | bytes 43024384 | tf_op jit(solution)/shard_map/convert_element_type | solution.py:165
  511.2 2.7 convolution_convert_fusion.7
  515.6 1.8 fusion.12
  519.0 3.2 convolution_convert_fusion.9
  523.3 3.2 convolution_convert_fusion.5
  527.1 98.8 %all-reduce.5.cloned.1.call-done = (bf16[8,4,32,768]{3,2,0,1:T(8,128)(2,1)}, bf16[256,1024]{1,0:T(8,128)(2,1)}, bf16[8,4,32,1024]{3,2,0,1:T(8,128)(2,1)}, bf16[1024,1024]{1,0:T(8,128)(2,1)}) async-done(((bf16[8,4,32,768]{3,2,0,1:T(8,128)(2,1)}, bf16[256,1024]{1,0:T(8,128)(2,1)}, bf16[8,4,32,1024]{3,2,0,1:T(8,128)(2,1)}, bf16[1024,1024]{1,0:T(8,128)(2,1)}), (bf16[8,4,32,768]{3,2,0,1:T(8,128)(2,1)}, ...) | async-done | bytes 6291472
  627.5 16.3 %all_to_all.16 = bf16[4,32,768]{2,1,0:T(8,128)(2,1)} all-to-all(bf16[4,32,768]{2,1,0:T(8,128)(2,1)S(1)} %dynamic-slice_bitcast_fusion.1), channel_id=1, replica_groups=mesh['replica'=8,'group'=4] {'group'}, dimensions={0} | all-to-all | bytes 393216 | tf_op jit(solution)/shard_map/all_to_all | solution.py:140
  645.5 17.5 %all_to_all.17 = bf16[4,32,1024]{2,1,0:T(8,128)(2,1)} all-to-all(bf16[4,32,1024]{2,1,0:T(8,128)(2,1)S(1)} %dynamic-slice_bitcast_fusion), channel_id=1, replica_groups=mesh['replica'=8,'group'=4] {'group'}, dimensions={0} | all-to-all | bytes 524288 | tf_op jit(solution)/shard_map/all_to_all | solution.py:140
  663.4 37.7 %psum.21 = f32[4,3072]{1,0:T(4,128)S(1)} all-reduce(f32[4,3072]{1,0:T(4,128)S(1)} %pad_maximum_fusion.4), channel_id=1, replica_groups=mesh['replica'=8,'group'=4] {'replica','group'}, use_global_device_ids=true, to_apply=%region_25.26 | all-reduce | flops 12288 | bytes 98304 | tf_op jit(solution)/shard_map/psum | solution.py:200
  702.5 2.1 convert_element_type.309
  704.6 4.1 convert_element_type.315
  708.7 2.0 add_convert_fusion.1
  710.7 5.6 reshape.304
  716.3 5.9 copy.78
  722.2 5.3 reshape.302
  727.5 7.4 all-gather.29.cloned.1.call-done
  735.0 2.1 convert_bitcast_fusion
  737.0 2.7 copy.79
  739.8 5.8 copy.88
  (171 shorter events, 36.0 us)
Async XLA Ops:
  7.2 264.8 %copy-start = (bf16[1024,1024]{1,0:T(8,128)(2,1)S(1)}, bf16[1024,1024]{1,0:T(8,128)(2,1)}, u32[]{:S(2)}) copy-start(bf16[1024,1024]{1,0:T(8,128)(2,1)} %param.26) | copy-start | bytes 6291460
  7.2 24.2 %copy-start.25 = (bf16[256]{0:T(256)(128)(2,1)S(1)}, bf16[256]{0:T(256)(128)(2,1)}, u32[]{:S(2)}) copy-start(bf16[256]{0:T(256)(128)(2,1)} %param.18) | copy-start | bytes 1540
  7.2 24.2 %copy-start.26 = (bf16[256]{0:T(256)(128)(2,1)S(1)}, bf16[256]{0:T(256)(128)(2,1)}, u32[]{:S(2)}) copy-start(bf16[256]{0:T(256)(128)(2,1)} %param.19) | copy-start | bytes 1540
  7.2 24.2 %copy-start.21 = (s32[1024]{0:T(1024)S(1)}, s32[1024]{0:T(1024)}, u32[]{:S(2)}) copy-start(s32[1024]{0:T(1024)} %param.30) | copy-start | bytes 12292
  7.2 48.3 %all-gather.23.cloned.1.call-start = ((), (), s32[]{:S(2)}) async-start(), calls=%async_computation.15 | async-start | bytes 1769472 | tf_op jit(solution)/shard_map/all_gather | solution.py:65
  30.6 72.5 %all-gather.15.cloned.1.call-start = ((), (), s32[]{:S(2)}) async-start(), calls=%async_computation.7 | async-start | bytes 2621440 | tf_op jit(solution)/shard_map/all_gather | solution.py:69
  31.4 146.9 %reduce-scatter.11.cloned.1.call-start = ((), (), s32[]{:S(2)}) async-start(), calls=%async_computation.8 | async-start | bytes 2621440 | tf_op jit(solution)/shard_map/reduce_scatter | solution.py:102
  107.1 8.3 %copy-start.8 = (bf16[1024,256]{0,1:T(8,128)(2,1)}, bf16[1024,256]{0,1:T(8,128)(2,1)S(1)}, u32[]{:S(2)}) copy-start(bf16[1024,256]{0,1:T(8,128)(2,1)S(1)} %slice.99) | copy-start | bytes 1572868
  108.1 7.3 copy-start.10
  124.2 9.0 %copy-start.17 = (bf16[256,1024]{1,0:T(8,128)(2,1)S(1)}, bf16[256,1024]{1,0:T(8,128)(2,1)}, u32[]{:S(2)}) copy-start(bf16[256,1024]{1,0:T(8,128)(2,1)} %param.20) | copy-start | bytes 1572868
  132.4 4.7 copy-start.27
  132.4 4.7 copy-start.28
  132.4 4.7 copy-start.29
  132.5 4.7 copy-start.30
  132.5 4.7 copy-start.31
  132.5 4.7 copy-start.32
  135.3 48.3 %copy-start.22 = (bf16[1024]{0:T(1024)(128)(2,1)S(1)}, bf16[1024]{0:T(1024)(128)(2,1)}, u32[]{:S(2)}) copy-start(bf16[1024]{0:T(1024)(128)(2,1)} %param.25) | copy-start | bytes 6148
  135.3 72.7 %all-gather.25.cloned.1.call-start = ((), (), s32[]{:S(2)}) async-start(), calls=%async_computation.16 | async-start | bytes 2359296 | tf_op jit(solution)/shard_map/all_gather | solution.py:65
  137.1 119.0 %all-gather.17.cloned.1.call-start = ((), (), s32[]{:S(2)}) async-start(), calls=%async_computation.9 | async-start | bytes 2621440 | tf_op jit(solution)/shard_map/all_gather | solution.py:107
  183.6 134.9 %reduce-scatter.13.cloned.1.call-start = ((), (), s32[]{:S(2)}) async-start(), calls=%async_computation.10 | async-start | bytes 2621440 | tf_op jit(solution)/shard_map/reduce_scatter | solution.py:102
  270.7 1.3 copy-start.36
  275.7 95.1 %all-gather.19.cloned.1.call-start = ((), (), s32[]{:S(2)}) async-start(), calls=%async_computation.11 | async-start | bytes 2621440 | tf_op jit(solution)/shard_map/all_gather | solution.py:107
  318.5 3.7 copy-start.14
  325.5 100.2 %reduce-scatter.15.cloned.1.call-start = ((), (), s32[]{:S(2)}) async-start(), calls=%async_computation.12 | async-start | bytes 2621440 | tf_op jit(solution)/shard_map/reduce_scatter | solution.py:102
  370.9 8.3 %copy-start.13 = (bf16[4,8,32,1024]{3,2,1,0:T(8,128)(2,1)S(1)}, bf16[4,8,32,1024]{3,2,1,0:T(8,128)(2,1)}, u32[]{:S(2)}) copy-start(bf16[4,8,32,1024]{3,2,1,0:T(8,128)(2,1)} %copy.73) | copy-start | bytes 6291460
  377.9 1.3 copy-start.37
  379.2 46.5 %copy-start.2 = (bf16[256,1024]{1,0:T(8,128)(2,1)S(1)}, bf16[256,1024]{1,0:T(8,128)(2,1)}, u32[]{:S(2)}) copy-start(bf16[256,1024]{1,0:T(8,128)(2,1)} %param.16) | copy-start | bytes 1572868
  379.2 46.5 %copy-start.3 = (bf16[256,1024]{1,0:T(8,128)(2,1)S(1)}, bf16[256,1024]{1,0:T(8,128)(2,1)}, u32[]{:S(2)}) copy-start(bf16[256,1024]{1,0:T(8,128)(2,1)} %reduce-scatter.11.cloned.1.call-done) | copy-start | bytes 1572868
  379.2 46.5 %copy-start.5 = (f32[256,1024]{1,0:T(8,128)S(1)}, f32[256,1024]{1,0:T(8,128)}, u32[]{:S(2)}) copy-start(f32[256,1024]{1,0:T(8,128)} %copy-done.4) | copy-start | bytes 3145732
  383.0 93.5 %all-gather.21.cloned.1.call-start = ((), (), s32[]{:S(2)}) async-start(), calls=%async_computation.13 | async-start | bytes 2621440 | tf_op jit(solution)/shard_map/all_gather | solution.py:107
  431.1 194.8 %all-reduce.5.cloned.1.call-start = ((), (), s32[]{:S(2)}) async-start(), calls=%async_computation.19 | async-start | bytes 12582912
  431.2 6.1 copy-start.24
  431.2 6.1 copy-start.38
  437.3 39.2 %copy-start.18 = (bf16[256,1024]{1,0:T(8,128)(2,1)S(1)}, bf16[256,1024]{1,0:T(8,128)(2,1)}, u32[]{:S(2)}) copy-start(bf16[256,1024]{1,0:T(8,128)(2,1)} %param.20) | copy-start | bytes 1572868
  478.8 8.2 %copy-start.12 = (bf16[1024,256]{0,1:T(8,128)(2,1)S(1)}, bf16[1024,256]{0,1:T(8,128)(2,1)}, u32[]{:S(2)}) copy-start(bf16[1024,256]{0,1:T(8,128)(2,1)} %get-tuple-element.40) | copy-start | bytes 1572868
  487.0 28.5 %copy-start.33 = (bf16[4,64,1024]{2,1,0:T(8,128)(2,1)}, bf16[4,64,1024]{2,1,0:T(8,128)(2,1)S(1)}, u32[]{:S(2)}) copy-start(bf16[4,64,1024]{2,1,0:T(8,128)(2,1)S(1)} %get-tuple-element.62) | copy-start | bytes 1572868
  499.1 12.1 %copy-start.11 = (bf16[1024,256]{0,1:T(8,128)(2,1)S(1)}, bf16[1024,256]{0,1:T(8,128)(2,1)}, u32[]{:S(2)}) copy-start(bf16[1024,256]{0,1:T(8,128)(2,1)} %copy-done.10) | copy-start | bytes 1572868
  511.2 2.7 copy-start.9
  513.8 1.7 copy-start.23
  515.5 3.5 copy-start.20
  519.0 3.5 copy-start.16
  522.2 1.0 copy-start.34
  522.2 4.3 copy-start.35
  522.3 186.4 %reduce-scatter.17.cloned.1.call-start = ((), (), s32[]{:S(2)}) async-start(), calls=%async_computation.14 | async-start | bytes 2621440 | tf_op jit(solution)/shard_map/reduce_scatter | solution.py:102
  526.4 184.3 %all-gather.27.cloned.1.call-start = ((), (), s32[]{:S(2)}) async-start(), calls=%async_computation.17 | async-start | bytes 1769472 | tf_op jit(solution)/shard_map/all_gather | solution.py:141
  643.8 91.1 %all-gather.29.cloned.1.call-start = ((), (), s32[]{:S(2)}) async-start(), calls=%async_computation.18 | async-start | bytes 2359296 | tf_op jit(solution)/shard_map/all_gather | solution.py:141
  663.0 45.7 %copy-start.7 = (f32[256,1024]{1,0:T(8,128)S(1)}, f32[256,1024]{1,0:T(8,128)}, u32[]{:S(2)}) copy-start(f32[256,1024]{1,0:T(8,128)} %copy-done.6) | copy-start | bytes 3145732
  739.8 5.9 copy-start.1
  (4 other events, 3.6 us)
Sparse Core Ops, SparseCore 0:
  30.7 24.7 all-gather.22
  57.1 45.9 all-gather.14
  135.4 42.7 reduce-scatter.10
  180.7 27.2 all-gather.24
  210.0 45.9 all-gather.16
  275.9 42.5 reduce-scatter.12
  325.6 45.2 all-gather.18
  383.1 42.5 reduce-scatter.14
  431.2 45.2 all-gather.20
  522.4 103.4 all-reduce.4
  628.8 48.3 reduce-scatter.16
  679.1 26.0 all-gather.26
  707.2 27.6 all-gather.28

commit v2 on v1

--- a/solution.py
+++ b/solution.py
@@ -1,6 +1,10 @@
+import functools
+
 import jax
 import jax.numpy as jnp
 from jax import lax
+from jax.experimental import pallas as pl
+from jax.experimental.pallas import tpu as pltpu
 from jax.sharding import PartitionSpec as P
 
 D = 1024
@@ -24,6 +28,247 @@
 
 def matmul(left, right):
     return jnp.dot(left, right, preferred_element_type=jnp.float32)
+
+
+MESH = pl.DeviceIdType.MESH
+EXTRA = 16
+
+
+def greet_neighbours(me, n):
+    barrier = pltpu.get_barrier_semaphore()
+
+    @pl.when(me > 0)
+    def _():
+        pl.semaphore_signal(
+            barrier, inc=1, device_id={"group": me - 1}, device_id_type=MESH
+        )
+
+    @pl.when(me < n - 1)
+    def _():
+        pl.semaphore_signal(
+            barrier, inc=1, device_id={"group": me + 1}, device_id_type=MESH
+        )
+
+    peers = jnp.where(me > 0, 1, 0) + jnp.where(me < n - 1, 1, 0)
+    pl.semaphore_wait(barrier, peers)
+
+
+def remote(src, dst, send, recv, target):
+    return pltpu.make_async_remote_copy(
+        src_ref=src,
+        dst_ref=dst,
+        send_sem=send,
+        recv_sem=recv,
+        device_id={"group": target},
+        device_id_type=MESH,
+    )
+
+
+def chunk_rows(rows, most):
+    step = rows // most if rows % (16 * most) == 0 else rows
+    return [(start, step) for start in range(0, rows, step)]
+
+
+def gather_kernel(n, cuts, x_ref, y_ref, xs_ref, ys_ref, send_sem, recv_sem):
+    me = lax.axis_index("group")
+    rows, extra = x_ref.shape[0], y_ref.shape[0]
+    pieces = [(xs_ref, rows, start, size) for start, size in cuts]
+    pieces.append((ys_ref, extra, 0, extra))
+    xs_ref[pl.ds(pl.multiple_of(me * rows, rows), rows)] = x_ref[...]
+    ys_ref[pl.ds(pl.multiple_of(me * extra, extra), extra)] = y_ref[...]
+    greet_neighbours(me, n)
+
+    def copy(way, block, at):
+        ref, height, start, size = pieces[at]
+        part = ref.at[pl.ds(pl.multiple_of(block * height + start, 16), size)]
+        target = me + 1 if way == 0 else me - 1
+        return remote(part, part, send_sem.at[way, block, at], recv_sem.at[block, at], target)
+
+    for step in range(n):
+        for at in range(len(pieces)):
+            for way in range(2):
+                block = me - step if way == 0 else me + step
+                there = block >= 0 if way == 0 else block < n
+                onward = me < n - 1 if way == 0 else me > 0
+                if step > 0:
+
+                    @pl.when(there)
+                    def _():
+                        copy(1 - way, block, at).wait_recv()
+
+                if step < n - 1:
+
+                    @pl.when(jnp.logical_and(there, onward))
+                    def _():
+                        copy(way, block, at).start()
+
+    for step in range(n - 1):
+        for at in range(len(pieces)):
+            for way in range(2):
+                block = me - step if way == 0 else me + step
+                there = block >= 0 if way == 0 else block < n
+                onward = me < n - 1 if way == 0 else me > 0
+
+                @pl.when(jnp.logical_and(there, onward))
+                def _():
+                    copy(way, block, at).wait_send()
+
+
+def gather_rows(rows, extra, place):
+    n = lax.axis_size("group")
+    cuts = chunk_rows(rows.shape[0], 4)
+    vmem = pl.BlockSpec(memory_space=pltpu.VMEM)
+    return pl.pallas_call(
+        functools.partial(gather_kernel, n, cuts),
+        out_shape=[
+            jax.ShapeDtypeStruct((n * rows.shape[0], rows.shape[1]), rows.dtype),
+            jax.ShapeDtypeStruct((n * extra.shape[0], extra.shape[1]), extra.dtype),
+        ],
+        in_specs=[vmem, vmem],
+        out_specs=[vmem, vmem],
+        scratch_shapes=[
+            pltpu.SemaphoreType.DMA((2, n, len(cuts) + 1)),
+            pltpu.SemaphoreType.DMA((n, len(cuts) + 1)),
+        ],
+        compiler_params=pltpu.CompilerParams(
+            collective_id=place, has_side_effects=True, vmem_limit_bytes=40 * 2**20
+        ),
+    )(rows, extra)
+
+
+def reduce_kernel(n, cuts, x_ref, out_ref, right_ref, left_ref, send_sem, recv_sem):
+    me = lax.axis_index("group")
+    rows = out_ref.shape[0]
+    greet_neighbours(me, n)
+
+    def copy(way, block, at):
+        start, size = cuts[at]
+        ref = right_ref if way == 0 else left_ref
+        part = ref.at[block, pl.ds(start, size)]
+        target = me + 1 if way == 0 else me - 1
+        return remote(part, part, send_sem.at[way, block, at], recv_sem.at[way, block, at], target)
+
+    for step in range(n - 1):
+        for at, (start, size) in enumerate(cuts):
+            for way in range(2):
+                block = n - 1 - step if way == 0 else step
+                ref = right_ref if way == 0 else left_ref
+                first = me == 0 if way == 0 else me == n - 1
+                passes = me < block if way == 0 else me > block
+                mine = x_ref[block * rows + start : block * rows + start + size]
+
+                @pl.when(jnp.logical_and(passes, first))
+                def _():
+                    ref[block, start : start + size] = mine
+
+                @pl.when(jnp.logical_and(passes, jnp.logical_not(first)))
+                def _():
+                    copy(way, block, at).wait_recv()
+                    held = ref[block, start : start + size].astype(jnp.float32)
+                    ref[block, start : start + size] = (
+                        held + mine.astype(jnp.float32)
+                    ).astype(ref.dtype)
+
+                @pl.when(passes)
+                def _():
+                    copy(way, block, at).start()
+
+    for at, (start, size) in enumerate(cuts):
+        own = pl.ds(pl.multiple_of(me * rows + start, 16), size)
+        out_ref[start : start + size] = x_ref[own].astype(jnp.float32)
+
+        @pl.when(me > 0)
+        def _():
+            copy(0, me, at).wait_recv()
+            out_ref[start : start + size] += right_ref[me, start : start + size].astype(
+                jnp.float32
+            )
+
+        @pl.when(me < n - 1)
+        def _():
+            copy(1, me, at).wait_recv()
+            out_ref[start : start + size] += left_ref[me, start : start + size].astype(
+                jnp.float32
+            )
+
+    for step in range(n - 1):
+        for at in range(len(cuts)):
+            for way in range(2):
+                block = n - 1 - step if way == 0 else step
+
+                @pl.when(me < block if way == 0 else me > block)
+                def _():
+                    copy(way, block, at).wait_send()
+
+
+def reduce_rows(terms, place):
+    n = lax.axis_size("group")
+    rows, width = terms.shape[0] // n, terms.shape[1]
+    cuts = chunk_rows(rows, 4)
+    vmem = pl.BlockSpec(memory_space=pltpu.VMEM)
+    return pl.pallas_call(
+        functools.partial(reduce_kernel, n, cuts),
+        out_shape=jax.ShapeDtypeStruct((rows, width), jnp.float32),
+        in_specs=[vmem],
+        out_specs=vmem,
+        scratch_shapes=[
+            pltpu.VMEM((n, rows, width), jnp.bfloat16),
+            pltpu.VMEM((n, rows, width), jnp.bfloat16),
+            pltpu.SemaphoreType.DMA((2, n, len(cuts))),
+            pltpu.SemaphoreType.DMA((2, n, len(cuts))),
+        ],
+        compiler_params=pltpu.CompilerParams(
+            collective_id=place, has_side_effects=True, vmem_limit_bytes=40 * 2**20
+        ),
+    )(terms.astype(jnp.bfloat16))
+
+
+def exchange_kernel(n, x_ref, out_ref, send_sem, recv_sem):
+    me = lax.axis_index("group")
+    barrier = pltpu.get_barrier_semaphore()
+    for hop in range(1, n):
+        pl.semaphore_signal(
+            barrier,
+            inc=1,
+            device_id={"group": lax.rem(me + hop, n)},
+            device_id_type=MESH,
+        )
+    pl.semaphore_wait(barrier, n - 1)
+    out_ref[me] = x_ref[me]
+    copies = []
+    for hop in range(1, n):
+        target = lax.rem(me + hop, n)
+        copy = remote(
+            x_ref.at[target], out_ref.at[me], send_sem.at[hop], recv_sem.at[hop], target
+        )
+        copy.start()
+        copies.append(copy)
+    for hop in range(1, n):
+        source = lax.rem(me + n - hop, n)
+        remote(
+            x_ref.at[source],
+            out_ref.at[source],
+            send_sem.at[hop],
+            recv_sem.at[hop],
+            source,
+        ).wait_recv()
+    for copy in copies:
+        copy.wait_send()
+
+
+def exchange(parts, place):
+    n = lax.axis_size("group")
+    vmem = pl.BlockSpec(memory_space=pltpu.VMEM)
+    return pl.pallas_call(
+        functools.partial(exchange_kernel, n),
+        out_shape=jax.ShapeDtypeStruct(parts.shape, parts.dtype),
+        in_specs=[vmem],
+        out_specs=vmem,
+        scratch_shapes=[pltpu.SemaphoreType.DMA((n,)), pltpu.SemaphoreType.DMA((n,))],
+        compiler_params=pltpu.CompilerParams(
+            collective_id=place, has_side_effects=True, vmem_limit_bytes=40 * 2**20
+        ),
+    )(parts)
 
 
 def on_device(
@@ -59,19 +304,20 @@
     qkv_rows = qkv_rows.reshape(piece, 3, groups, own).transpose(2, 0, 1, 3)
     inner_rows = inner_rows.reshape(piece, groups, hidden).transpose(1, 0, 2)
     moved = jnp.concatenate([qkv_rows.reshape(groups, piece, 3 * own), inner_rows], axis=2)
-    moved = lax.all_to_all(moved, "group", split_axis=0, concat_axis=0, tiled=True)
+    moved = exchange(moved, 0)
 
     def spread(shares):
         every = lax.all_gather(shares, "replica", axis=0)
         return every.transpose(1, 0, 2, 3).reshape(D, shares.shape[-1])
 
     qkv_cols = spread(moved[:, :, : 3 * own])
-    input_all = lax.all_gather(layer_input, "group", axis=0, tiled=True)
     inner_cols = spread(moved[:, :, 3 * own :])
     vectors = jnp.stack(
         [attn_bias, first_gain, first_shift, outer_bias, second_gain, second_shift]
     )
-    vectors = lax.all_gather(vectors, "group", axis=0).transpose(1, 0, 2).reshape(6, D)
+    vectors = jnp.pad(vectors, ((0, EXTRA - 6), (0, 0)))
+    input_all, vectors = gather_rows(layer_input, vectors, 1)
+    vectors = vectors.reshape(groups, EXTRA, own)[:, :6].transpose(1, 0, 2).reshape(6, D)
     attn_bias_full, gain_one, shift_one, outer_bias_full, gain_two, shift_two = vectors
 
     projected = matmul(input_all, qkv_cols)
@@ -98,24 +344,30 @@
     )
     attended = attended.reshape(length, own).astype(jnp.bfloat16)
 
-    def to_owner(terms):
-        return lax.psum_scatter(
-            terms.astype(jnp.bfloat16), "group", scatter_dimension=0, tiled=True
-        ).astype(jnp.float32)
-
-    def to_all(rows):
-        return lax.all_gather(rows, "group", axis=0, tiled=True)
-
-    branch = to_owner(matmul(attended, attn_weight)) + attn_bias_full
+    def own_sums(extra):
+        sums = jnp.sum(extra.reshape(groups, EXTRA, D)[:, :2].astype(jnp.float32), axis=0)
+        return lax.dynamic_slice_in_dim(sums, group_place * own, own, axis=1)
+
+    def own_columns(rows):
+        columns = lax.dynamic_slice_in_dim(rows, group_place * own, own, axis=1)
+        return jnp.sum(columns.astype(jnp.float32), axis=0)
+
+    def extra_rows(values, width):
+        values = jnp.concatenate(values).astype(jnp.bfloat16)
+        values = jnp.pad(values, (0, EXTRA * width - values.shape[0]))
+        return values.reshape(EXTRA, width)
+
+    branch = reduce_rows(matmul(attended, attn_weight), 2) + attn_bias_full
     residual_one = layer_input.astype(jnp.float32) + branch
     first, first_pull = jax.vjp(
         layer_norm, residual_one, gain_one.astype(jnp.float32), shift_one.astype(jnp.float32)
     )
-    first_all = to_all(first.astype(jnp.bfloat16))
+    empty = jnp.zeros((EXTRA, 128), jnp.bfloat16)
+    first_all, _ = gather_rows(first.astype(jnp.bfloat16), empty, 3)
     inner = matmul(first_all, inner_cols) + inner_bias
     activated_f, gelu_pull = jax.vjp(gelu_exact, inner)
     activated = activated_f.astype(jnp.bfloat16)
-    outer = to_owner(matmul(activated, outer_weight)) + outer_bias_full
+    outer = reduce_rows(matmul(activated, outer_weight), 4) + outer_bias_full
     result, second_pull = jax.vjp(
         layer_norm, first + outer, gain_two.astype(jnp.float32), shift_two.astype(jnp.float32)
     )
@@ -124,34 +376,38 @@
         output_grad.astype(jnp.float32)
     )
     outer_grad = second_res_grad.astype(jnp.bfloat16)
-    outer_bias_grad = jnp.sum(outer_grad.astype(jnp.float32), axis=0)
-    outer_all = to_all(outer_grad)
+    outer_all, second_extra = gather_rows(
+        outer_grad, extra_rows([second_gain_grad, second_shift_grad], D), 5
+    )
     inner_grad = gelu_pull(matmul(outer_all, outer_weight.T))[0].astype(jnp.bfloat16)
     inner_bias_grad = jnp.sum(inner_grad.astype(jnp.float32), axis=0)
-    first_grad = second_res_grad + to_owner(matmul(inner_grad, inner_cols.T))
     outer_weight_grad = matmul(activated.T, outer_all).astype(jnp.bfloat16)
-    outer_weight_grad = lax.psum(outer_weight_grad, "replica").astype(jnp.float32)
-
-    def to_rows(columns):
-        width = columns.shape[-1]
-        parts = columns.astype(jnp.bfloat16).reshape(groups, replicas, piece, width)
-        parts = parts.transpose(1, 0, 2, 3)
-        summed = lax.psum_scatter(parts, "replica", scatter_dimension=0)
-        summed = lax.all_to_all(summed, "group", split_axis=0, concat_axis=0, tiled=True)
-        return lax.all_gather(summed, "replica", axis=0)
-
-    inner_weight_grad = to_rows(matmul(first_all.T, inner_grad))
-    inner_weight_grad = inner_weight_grad.transpose(0, 2, 1, 3).reshape(own, groups * hidden)
-    inner_weight_grad = inner_weight_grad.astype(jnp.float32)
+    early = extra_rows(
+        [own_sums(second_extra).reshape(-1), own_columns(outer_all), inner_bias_grad], D
+    )
+    inner_weight_grad = matmul(first_all.T, inner_grad).astype(jnp.bfloat16)
+    outer_weight_grad, inner_weight_grad = lax.psum(
+        (jnp.concatenate([outer_weight_grad, early], axis=0), inner_weight_grad), "replica"
+    )
+
+    def to_rows(columns, place):
+        parts = columns.reshape(groups, replicas, piece, columns.shape[-1])
+        parts = lax.dynamic_index_in_dim(parts, replica_place, axis=1, keepdims=False)
+        return lax.all_gather(exchange(parts, place), "replica", axis=0)
+
+    inner_rows_grad = to_rows(inner_weight_grad, 6)
+    inner_rows_grad = inner_rows_grad.transpose(0, 2, 1, 3).reshape(own, groups * hidden)
+    inner_rows_grad = inner_rows_grad.astype(jnp.float32)
+    first_grad = second_res_grad + reduce_rows(matmul(inner_grad, inner_cols.T), 7)
 
     first_res_grad, first_gain_grad, first_shift_grad = first_pull(first_grad)
     branch_grad = first_res_grad.astype(jnp.bfloat16)
-    attn_bias_grad = jnp.sum(branch_grad.astype(jnp.float32), axis=0)
-    branch_all = to_all(branch_grad)
+    branch_all, first_extra = gather_rows(
+        branch_grad, extra_rows([first_gain_grad, first_shift_grad], D), 8
+    )
     attended_grad = matmul(branch_all, attn_weight.T).astype(jnp.bfloat16)
     attended_grad = attended_grad.reshape(length, heads, HD)
     attn_weight_grad = matmul(attended.T, branch_all).astype(jnp.bfloat16)
-    attn_weight_grad = lax.psum(attn_weight_grad, "replica").astype(jnp.float32)
 
     probs = jnp.exp(masked_scores() - log_total)
     probs_low = probs.astype(jnp.bfloat16)
@@ -174,48 +430,52 @@
     keys_grad = keys_grad.reshape(length, own).astype(jnp.bfloat16)
     values_grad = values_grad.reshape(length, own).astype(jnp.bfloat16)
     projected_grad = jnp.concatenate([scaled_queries, keys_grad, values_grad], axis=1)
-    input_terms = to_owner(matmul(projected_grad, qkv_cols.T))
+    query_bias_grad = jnp.sum(scaled_queries.astype(jnp.float32), axis=0)
+    value_bias_grad = jnp.sum(values_grad.astype(jnp.float32), axis=0)
+    late = extra_rows(
+        [
+            own_sums(first_extra).reshape(-1),
+            own_columns(branch_all),
+            query_bias_grad,
+            value_bias_grad,
+        ],
+        D,
+    )
+    attn_weight_grad = jnp.concatenate([attn_weight_grad, late], axis=0)
+    last_grad, _, outer_weight_grad = lax.optimization_barrier(
+        (projected_grad, inner_weight_grad, outer_weight_grad)
+    )
+    qkv_weight_grad = matmul(input_all.T, last_grad).astype(jnp.bfloat16)
+    qkv_weight_grad, attn_weight_grad = lax.psum((qkv_weight_grad, attn_weight_grad), "replica")
+    input_terms = reduce_rows(matmul(projected_grad, qkv_cols.T), 9)
     input_grad = (first_res_grad + input_terms).astype(jnp.bfloat16)
-    qkv_weight_grad = to_rows(matmul(input_all.T, projected_grad))
+    early = outer_weight_grad[hidden:].reshape(-1).astype(jnp.float32)
+    outer_weight_grad = outer_weight_grad[:hidden].astype(jnp.float32)
+    late = attn_weight_grad[own:].reshape(-1).astype(jnp.float32)
+    attn_weight_grad = attn_weight_grad[:own].astype(jnp.float32)
+    qkv_weight_grad = to_rows(qkv_weight_grad, 10)
     qkv_weight_grad = qkv_weight_grad.reshape(replicas, groups, piece, 3, own)
     qkv_weight_grad = qkv_weight_grad.transpose(0, 2, 3, 1, 4).reshape(own, 3 * D)
     qkv_weight_grad = qkv_weight_grad.astype(jnp.float32)
-
-    query_bias_grad = jnp.sum(scaled_queries.astype(jnp.float32), axis=0)
-    value_bias_grad = jnp.sum(values_grad.astype(jnp.float32), axis=0)
-    shared = jnp.stack(
-        [
-            attn_bias_grad,
-            first_gain_grad,
-            first_shift_grad,
-            outer_bias_grad,
-            second_gain_grad,
-            second_shift_grad,
-        ]
-    )
-    shared = shared.reshape(6, groups, own).transpose(1, 0, 2).reshape(groups, 6 * own)
-    mine = jnp.concatenate([query_bias_grad, value_bias_grad, inner_bias_grad])
-    is_mine = jnp.arange(groups)[:, None] == group_place
-    terms = jnp.concatenate([shared, jnp.where(is_mine, mine[None], 0.0)], axis=1)
-    terms = lax.psum(terms, ("replica", "group"))
-    terms = lax.dynamic_index_in_dim(terms, group_place, keepdims=False)
-    small = terms[: 8 * own].reshape(8, own)
+    second_gain_grad, second_shift_grad, outer_bias_grad = early[: 3 * own].reshape(3, own)
+    inner_bias_grad = early[3 * own : 3 * own + hidden]
+    late = late[: 5 * own].reshape(5, own)
     return (
         layer_output,
         input_grad,
         qkv_weight_grad,
-        small[6],
-        small[7],
+        late[3],
+        late[4],
         attn_weight_grad,
-        small[0],
-        small[1],
-        small[2],
-        inner_weight_grad,
-        terms[8 * own :],
+        late[2],
+        late[0],
+        late[1],
+        inner_rows_grad,
+        inner_bias_grad,
         outer_weight_grad,
-        small[3],
-        small[4],
-        small[5],
+        outer_bias_grad,
+        second_gain_grad,
+        second_shift_grad,
     )
 
 

time: 762 us -> 639 us (0.84)
  waiting for transfers between devices: 438 us -> 77.3 us
  Pallas kernels: 0 us -> 344 us
  blocking collectives: 104 us -> 0 us
    pallas_call x0 -> x11, Pallas kernels: none -> 344 us  [the longest x4 189 us: reduce_rows(): pl.pallas_call(functools.partial(reduce_kernel, n, cuts), out_shape=jax.S...]
    all_gather x6 -> x2, waiting for transfers between devices: 178 us -> 0.01 us  [to_rows(): return lax.all_gather(exchange(parts, place), 'replica', axis=0)]
    reduce_scatter x4 -> x0, waiting for transfers between devices: 113 us -> none  [to_owner(): lax.psum_scatter(terms.astype(jnp.bfloat16), 'group', scatter_dimension=0...]
    unnamed x14 -> x6, waiting for transfers between devices: 99.7 us -> 0.1 us
    psum x0 -> x2, waiting for transfers between devices: none -> 77.1 us  [the longest x1 51.6 us: on_device(): lax.psum((qkv_weight_grad, attn_weight_grad), 'replica')]
    all_to_all x3 -> x0, blocking collectives: 53 us -> none  [the longest x2 33.8 us: to_rows(): lax.all_to_all(summed, 'group', split_axis=0, concat_axis=0, tiled=True)]
    all_gather x2, waiting for transfers between devices: 47.8 us -> 0.04 us  [spread(): every = lax.all_gather(shares, 'replica', axis=0)]
    psum x1 -> x0, blocking collectives: 37.7 us -> none  [on_device(): terms = lax.psum(terms, ('replica', 'group'))]
  transfers between devices with their start and end apart: 13 -> 6, of which waited for: 11 -> 2; matrix products, arithmetic and copies ran while one was open for 8% -> 18% of each run, Pallas kernels for 0% -> 29%
where the time goes in v2:
time: 639 us; the launch traced here: 627 us
  Pallas kernels  344 us (54%)
  matrix products  95.8 us (15%)
  waiting for transfers between devices  77.3 us (12%)
  other arithmetic  47.3 us (7%)
  local copies, waits for them, and re-layouts  47.1 us (7%)
  between operations  15.3 us (2%)
    pallas_call x4, Pallas kernels, reduce_rows(): pl.pallas_call(functools.partial(reduce_kernel, n, cuts), out_shape=jax.S...  189 us
    pallas_call x4, Pallas kernels, gather_rows(): pl.pallas_call(functools.partial(gather_kernel, n, cuts), out_shape=[jax....  124 us
    psum x1, waiting for transfers between devices, on_device(): lax.psum((qkv_weight_grad, attn_weight_grad), 'replica')  51.6 us
    dot_general x12, matrix products, matmul(): return jnp.dot(left, right, preferred_element_type=jnp.float32)  46.9 us
    pallas_call x3, Pallas kernels, exchange(): pl.pallas_call(functools.partial(exchange_kernel, n), out_shape=jax.Shape...  30.5 us
    psum x1, waiting for transfers between devices, on_device(): lax.psum((jnp.concatenate([outer_weight_grad, early], axis=0), inner_weig...  25.5 us
    convert_element_type x3, local copies, waits for them, and re-layouts, on_device(): qkv_weight_grad = qkv_weight_grad.astype(jnp.float32)  16.8 us
    convert_element_type x1, other arithmetic, on_device(): scores_grad = (probs * (probs_grad - weighted)).astype(jnp.bfloat16)  16.2 us
  transfers between devices with their start and end apart: 6, of which 2 were waited for; matrix products, arithmetic and copies ran while one was open for 18% of the time, Pallas kernels for 29%

profile of v2, /device:TPU:0, one launch (start us, length us, event | category | flops | bytes accessed | tf_op | source)
XLA Modules:
  0.0 627.2 jit_solution(15758148282131855901)
XLA Ops:
  10.0 13.5 %shard_map.272 = bf16[4,32,1792]{2,1,0:T(8,128)(2,1)S(1)} custom-call(bf16[4,32,1792]{2,1,0:T(8,128)(2,1)S(1)} %pad_maximum_fusion.3.x_ref), custom_call_target="tpu_custom_call" | custom-call | tf_op jit(solution)/shard_map/pallas_call | solution.py:262
  26.5 1.6 broadcast_compare_fusion
  28.1 38.7 %shard_map.271 = (bf16[1024,1024]{1,0:T(8,128)(2,1)S(1)}, bf16[64,256]{1,0:T(8,128)(2,1)S(1)}) custom-call(bf16[256,1024]{1,0:T(8,128)(2,1)S(1)} %copy-done.2, bf16[16,256]{1,0:T(8,128)(2,1)S(1)} %pad.19.y_ref), custom_call_target="tpu_custom_call" | custom-call | tf_op jit(solution)/shard_map/pallas_call | solution.py:121
  68.2 1.5 copy.74
  69.7 4.0 fusion.60
  74.1 1.4 copy-done.9
  75.5 7.4 %select_reduce_fusion = (f32[4,1024]{1,0:T(4,128)S(1)}, f32[4,1024,1024]{1,2,0:T(8,128)}) fusion(pred[1024,1024]{0,1:T(8,128)(4,1)S(1)} %copy-done.9, bf16[1024,4,64]{0,2,1:T(8,128)(2,1)S(1)} %bitcast.112, bf16[1024,4,64]{0,2,1:T(8,128)(2,1)S(1)} %bitcast.110), kind=kOutput, calls=%fused_computation.6 | convolution fusion | flops 545255424 | bytes 18890752 | tf_op jit(solution)/shard_map/qhd,khd->hqk/dot_general | solution.py:333
  82.9 9.0 %fusion = f32[4,1024]{1,0:T(4,128)S(1)} fusion(f32[4,1024,1024]{1,2,0:T(8,128)} %get-tuple-element.73, f32[4,1024]{1,0:T(4,128)S(1)} %get-tuple-element.72, pred[1024,1024]{0,1:T(8,128)(4,1)} %broadcast_compare_fusion), kind=kLoop, calls=%fused_computation.5 | loop fusion | flops 12578816 | bytes 17858560 | tf_op jit(solution)/shard_map/reduce_sum | solution.py:339
  91.9 8.4 %fusion.18 = bf16[4,64,1024]{2,1,0:T(8,128)(2,1)S(1)} fusion(bf16[1024,4,64]{0,2,1:T(8,128)(2,1)S(1)} %bitcast.115, f32[4,1024,1024]{1,2,0:T(8,128)} %get-tuple-element.73, f32[4,1024]{1,0:T(4,128)S(1)} %fusion, f32[4,1024]{1,0:T(4,128)S(1)} %get-tuple-element.72, pred[1024,1024]{0,1:T(8,128)(4,1)} %broadcast_compare_fusion), kind=kOutput, calls=%fused_computation.52 | convolution fusion | flops 553910272 | bytes 18907136 | tf_op jit(solution)/shard_map/hqk,khd->qhd/dot_general | solution.py:342
  101.9 45.7 %shard_map.273 = f32[256,1024]{1,0:T(8,128)S(1)} custom-call(bf16[1024,1024]{1,0:T(8,128)(2,1)S(1)} %convolution_convert_fusion.4.x_ref), custom_call_target="tpu_custom_call" | custom-call | tf_op jit(solution)/shard_map/pallas_call | solution.py:209
  148.8 33.5 %shard_map.274 = (bf16[1024,1024]{1,0:T(8,128)(2,1)S(1)}, bf16[64,128]{1,0:T(8,128)(2,1)}) custom-call(bf16[256,1024]{1,0:T(8,128)(2,1)S(1)} %fusion.26.x_ref, bf16[16,128]{1,0:T(8,128)(2,1)S(1)} %broadcast_in_dim.28.y_ref), custom_call_target="tpu_custom_call" | custom-call | tf_op jit(solution)/shard_map/pallas_call | solution.py:121
  182.3 1.3 copy-done.6
  183.6 1.9 copy.76
  185.8 12.3 %multiply_convert_fusion.1 = (bf16[1024,1024]{1,0:T(8,128)(2,1)S(1)}, f32[1024,1024]{1,0:T(8,128)}, f32[1024,1024]{1,0:T(8,128)}) fusion(f32[1024]{0:T(1024)S(1)} %convert_element_type.280, bf16[1024,1024]{1,0:T(8,128)(2,1)S(1)} %copy-done.7, bf16[1024,1024]{1,0:T(8,128)(2,1)S(1)} %bitcast.119), kind=kOutput, calls=%fused_computation.15 | convolution fusion | flops 2216689664 | bytes 14684160 | tf_op jit(solution)/shard_map/dot_general | solution.py:30
  198.2 1.3 copy-done.42
  199.5 2.3 convolution_convert_fusion.3.x_ref
  201.9 48.2 %shard_map.275 = f32[256,1024]{1,0:T(8,128)S(1)} custom-call(bf16[1024,1024]{1,0:T(8,128)(2,1)S(1)} %convolution_convert_fusion.3.x_ref), custom_call_target="tpu_custom_call" | custom-call | tf_op jit(solution)/shard_map/pallas_call | solution.py:209
  251.5 2.8 fusion.53
  254.4 25.9 %shard_map.276 = (bf16[1024,1024]{1,0:T(8,128)(2,1)S(1)}, bf16[64,1024]{1,0:T(8,128)(2,1)S(1)}) custom-call(bf16[256,1024]{1,0:T(8,128)(2,1)S(1)} %add_convert_fusion.4.x_ref, bf16[16,1024]{1,0:T(8,128)(2,1)S(1)} %reshape.306.y_ref), custom_call_target="tpu_custom_call" | custom-call | tf_op jit(solution)/shard_map/pallas_call | solution.py:121
  280.4 6.4 %fusion.51 = (bf16[1024]{0:T(1024)(128)(2,1)S(1)}, bf16[1024,1024]{1,0:T(8,128)(2,1)S(1)}) fusion(f32[1024,1024]{1,0:T(8,128)S(1)} %copy-done.44, f32[1024,1024]{1,0:T(8,128)} %get-tuple-element.74, f32[1024]{0:T(1024)S(1)} %convert_element_type.280, bf16[1024,1024]{1,0:T(8,128)(2,1)S(1)} %get-tuple-element.27, bf16[1024,1024]{1,0:T(8,128)(2,1)S(1)} %copy-done), kind=kOutput, calls=%fused_computation.136 | convolution fusion | flops 2164259840 | bytes 14686208 | tf_op jit(solution)/shard_map/dot_general | solution.py:30
  286.8 3.8 convolution_convert_fusion.1
  290.6 2.4 convolution_convert_fusion.2.x_ref
  293.0 3.7 convolution_convert_fusion
  296.7 45.1 %shard_map.277 = f32[256,1024]{1,0:T(8,128)S(1)} custom-call(bf16[1024,1024]{1,0:T(8,128)(2,1)S(1)} %convolution_convert_fusion.2.x_ref), custom_call_target="tpu_custom_call" | custom-call | tf_op jit(solution)/shard_map/pallas_call | solution.py:209
  343.9 26.4 %shard_map.278 = (bf16[1024,1024]{1,0:T(8,128)(2,1)S(1)}, bf16[64,1024]{1,0:T(8,128)(2,1)S(1)}) custom-call(bf16[256,1024]{1,0:T(8,128)(2,1)S(1)} %add_convert_fusion.3.x_ref, bf16[16,1024]{1,0:T(8,128)(2,1)S(1)} %reshape.307.y_ref), custom_call_target="tpu_custom_call" | custom-call | tf_op jit(solution)/shard_map/pallas_call | solution.py:121
  370.3 2.6 convolution_convert_fusion.10
  374.2 3.2 pad_maximum_fusion
  378.0 12.8 %multiply_reduce_fusion = (f32[4,1024]{1,0:T(4,128)S(1)}, f32[4,1024,1024]{1,2,0:T(8,128)}) fusion(f32[4,1024,1024]{1,2,0:T(8,128)} %get-tuple-element.73, f32[4,1024]{1,0:T(4,128)S(1)} %log_add_fusion, pred[1024,1024]{0,1:T(8,128)(4,1)S(1)} %copy-done.10, bf16[1024,4,64]{0,2,1:T(8,128)(2,1)} %bitcast.132, bf16[1024,4,64]{0,2,1:T(8,128)(2,1)} %bitcast.116), kind=kOutput, calls=%fused_computation.1 | convolution fusion | flops 553644032 | bytes 35684352 | tf_op jit(solution)/shard_map/qhd,khd->hqk/dot_general | solution.py:414
  390.7 16.2 %multiply_convert_fusion = bf16[4,1024,1024]{1,2,0:T(8,128)(2,1)} fusion(f32[4,1024,1024]{1,2,0:T(8,128)} %get-tuple-element.76, f32[4,1024,1024]{1,2,0:T(8,128)} %get-tuple-element.73, f32[4,1024]{1,0:T(4,128)S(1)} %get-tuple-element.75, f32[4,1024]{1,0:T(4,128)S(1)} %log_add_fusion, pred[1024,1024]{0,1:T(8,128)(4,1)S(1)} %copy-done.10), kind=kLoop, calls=%fused_computation | loop fusion | flops 20971520 | bytes 43024384 | tf_op jit(solution)/shard_map/convert_element_type | solution.py:421
  406.9 8.9 %fusion.59 = (bf16[4,64]{1,0:T(4,128)(2,1)S(1)}, bf16[4,64,1024]{2,1,0:T(8,128)(2,1)}) fusion(bf16[1024,4,64]{0,2,1:T(8,128)(2,1)S(1)} %bitcast.133, f32[4,1024,1024]{1,2,0:T(8,128)} %get-tuple-element.73, f32[4,1024]{1,0:T(4,128)S(1)} %log_add_fusion, pred[1024,1024]{0,1:T(8,128)(4,1)S(1)} %copy-done.10), kind=kOutput, calls=%fused_computation.143 | convolution fusion | flops 549977856 | bytes 18891264 | tf_op jit(solution)/shard_map/hqk,qhd->khd/dot_general | solution.py:417
  415.9 5.2 bitcast_reduce_fusion
  421.2 1.8 convolution_convert_fusion.9
  423.9 6.3 %convolution_convert_fusion.7 = bf16[4,64,1024]{2,1,0:T(8,128)(2,1)S(1)} fusion(bf16[1024,4,64]{0,2,1:T(8,128)(2,1)S(1)} %bitcast.113, bf16[4,1024,1024]{1,2,0:T(8,128)(2,1)} %multiply_convert_fusion), kind=kOutput, calls=%fused_computation.45 | convolution fusion | flops 537133056 | bytes 9437184 | tf_op jit(solution)/shard_map/hqk,qhd->khd/dot_general | solution.py:425
  431.0 1.3 pad_maximum_fusion.1
  432.3 25.5 %all-reduce.12.cloned.1.call-done = (bf16[1024,1024]{1,0:T(8,128)(2,1)}, bf16[1040,1024]{1,0:T(8,128)(2,1)}) async-done(((bf16[1024,1024]{1,0:T(8,128)(2,1)}, bf16[1040,1024]{1,0:T(8,128)(2,1)}), (bf16[1024,1024]{1,0:T(8,128)(2,1)}, bf16[1040,1024]{1,0:T(8,128)(2,1)})) %all-reduce.12.cloned.1.call-update) | async-done | bytes 4227088 | tf_op jit(solution)/shard_map/psum | solution.py:389
  457.9 3.3 convolution_convert_fusion.6
  463.4 9.4 %shard_map.281 = bf16[4,32,1024]{2,1,0:T(8,128)(2,1)} custom-call(bf16[4,32,1024]{2,1,0:T(8,128)(2,1)S(1)} %dynamic-slice_bitcast_fusion.x_ref), custom_call_target="tpu_custom_call" | custom-call | tf_op jit(solution)/shard_map/pallas_call | solution.py:262
  473.1 51.6 %all-reduce.10.cloned.1.call-done = (bf16[4,8,32,768]{3,2,0,1:T(8,128)(2,1)}, bf16[272,1024]{1,0:T(8,128)(2,1)}) async-done(((bf16[4,8,32,768]{3,2,0,1:T(8,128)(2,1)}, bf16[272,1024]{1,0:T(8,128)(2,1)}), (bf16[4,8,32,768]{3,2,0,1:T(8,128)(2,1)}, bf16[272,1024]{1,0:T(8,128)(2,1)})) %all-reduce.10.cloned.1.call-update) | async-done | bytes 2129936 | tf_op jit(solution)/shard_map/psum | solution.py:449
  525.6 7.6 %shard_map.280 = bf16[4,32,768]{2,1,0:T(8,128)(2,1)} custom-call(bf16[4,32,768]{2,1,0:T(8,128)(2,1)S(1)} %dynamic-slice_bitcast_fusion.1.x_ref), custom_call_target="tpu_custom_call" | custom-call | tf_op jit(solution)/shard_map/pallas_call | solution.py:262
  533.3 3.5 convolution_convert_fusion.5.x_ref
  536.9 49.5 %shard_map.279 = f32[256,1024]{1,0:T(8,128)S(1)} custom-call(bf16[1024,1024]{1,0:T(8,128)(2,1)S(1)} %convolution_convert_fusion.5.x_ref), custom_call_target="tpu_custom_call" | custom-call | tf_op jit(solution)/shard_map/pallas_call | solution.py:209
  588.6 2.5 slice_convert_fusion
  592.8 2.1 convert_bitcast_fusion
  594.9 2.7 copy.83
  597.6 5.8 copy.93
  603.4 5.6 reshape.327
  609.0 6.1 copy.81
  615.0 5.1 reshape.323
  (178 shorter events, 24.7 us)
Async XLA Ops:
  7.2 192.3 %copy-start = (bf16[1024,1024]{1,0:T(8,128)(2,1)S(1)}, bf16[1024,1024]{1,0:T(8,128)(2,1)}, u32[]{:S(2)}) copy-start(bf16[1024,1024]{1,0:T(8,128)(2,1)} %param.26) | copy-start | bytes 6291460
  7.2 17.9 %copy-start.34 = (bf16[256]{0:T(256)(128)(2,1)S(1)}, bf16[256]{0:T(256)(128)(2,1)}, u32[]{:S(2)}) copy-start(bf16[256]{0:T(256)(128)(2,1)} %param.18) | copy-start | bytes 1540
  7.2 17.9 %copy-start.35 = (bf16[256]{0:T(256)(128)(2,1)S(1)}, bf16[256]{0:T(256)(128)(2,1)}, u32[]{:S(2)}) copy-start(bf16[256]{0:T(256)(128)(2,1)} %param.19) | copy-start | bytes 1540
  7.2 17.9 %copy-start.36 = (bf16[256]{0:T(256)(128)(2,1)S(1)}, bf16[256]{0:T(256)(128)(2,1)}, u32[]{:S(2)}) copy-start(bf16[256]{0:T(256)(128)(2,1)} %param.21) | copy-start | bytes 1540
  7.2 17.9 %copy-start.37 = (bf16[256]{0:T(256)(128)(2,1)S(1)}, bf16[256]{0:T(256)(128)(2,1)}, u32[]{:S(2)}) copy-start(bf16[256]{0:T(256)(128)(2,1)} %param.22) | copy-start | bytes 1540
  7.2 17.9 %copy-start.38 = (bf16[256]{0:T(256)(128)(2,1)S(1)}, bf16[256]{0:T(256)(128)(2,1)}, u32[]{:S(2)}) copy-start(bf16[256]{0:T(256)(128)(2,1)} %param.23) | copy-start | bytes 1540
  7.3 18.0 %copy-start.39 = (bf16[256]{0:T(256)(128)(2,1)S(1)}, bf16[256]{0:T(256)(128)(2,1)}, u32[]{:S(2)}) copy-start(bf16[256]{0:T(256)(128)(2,1)} %param.27) | copy-start | bytes 1540
  7.3 18.0 %copy-start.40 = (bf16[256]{0:T(256)(128)(2,1)S(1)}, bf16[256]{0:T(256)(128)(2,1)}, u32[]{:S(2)}) copy-start(bf16[256]{0:T(256)(128)(2,1)} %param.28) | copy-start | bytes 1540
  7.3 18.0 %copy-start.41 = (bf16[256]{0:T(256)(128)(2,1)S(1)}, bf16[256]{0:T(256)(128)(2,1)}, u32[]{:S(2)}) copy-start(bf16[256]{0:T(256)(128)(2,1)} %param.29) | copy-start | bytes 1540
  7.3 18.0 %copy-start.33 = (bf16[1024]{0:T(1024)(128)(2,1)S(1)}, bf16[1024]{0:T(1024)(128)(2,1)}, u32[]{:S(2)}) copy-start(bf16[1024]{0:T(1024)(128)(2,1)} %param.25) | copy-start | bytes 6148
  7.3 19.2 %copy-start.32 = (s32[1024]{0:T(1024)S(1)}, s32[1024]{0:T(1024)}, u32[]{:S(2)}) copy-start(s32[1024]{0:T(1024)} %param.30) | copy-start | bytes 12292
  7.3 20.8 %copy-start.2 = (bf16[256,1024]{1,0:T(8,128)(2,1)S(1)}, bf16[256,1024]{1,0:T(8,128)(2,1)}, u32[]{:S(2)}) copy-start(bf16[256,1024]{1,0:T(8,128)(2,1)} %x_ref.1) | copy-start | bytes 1572868
  7.3 60.8 %all-gather.9.cloned.1.call-start = ((), (), s32[]{:S(2)}) async-start(), calls=%async_computation | async-start | bytes 1769472 | tf_op jit(solution)/shard_map/all_gather | solution.py:310
  24.2 159.4 %all-gather.11.cloned.1.call-start = ((), (), s32[]{:S(2)}) async-start(), calls=%async_computation.1 | async-start | bytes 2359296 | tf_op jit(solution)/shard_map/all_gather | solution.py:310
  25.0 432.8 %all-reduce.12.cloned.1.call-start = ((), (), s32[]{:S(2)}) async-start(), calls=%async_computation.5 | async-start | bytes 8454144 | tf_op jit(solution)/shard_map/psum | solution.py:389
  66.8 1.3 copy-start.4
  69.7 4.1 copy-start.26
  73.8 1.7 copy-start.9
  73.9 9.0 %copy-start.16 = (bf16[1024,256]{0,1:T(8,128)(2,1)}, bf16[1024,256]{0,1:T(8,128)(2,1)S(1)}, u32[]{:S(2)}) copy-start(bf16[1024,256]{0,1:T(8,128)(2,1)S(1)} %slice.127) | copy-start | bytes 1572868
  74.1 8.8 %copy-start.17 = (bf16[1024,256]{0,1:T(8,128)(2,1)}, bf16[1024,256]{0,1:T(8,128)(2,1)S(1)}, u32[]{:S(2)}) copy-start(bf16[1024,256]{0,1:T(8,128)(2,1)S(1)} %get-tuple-element.55) | copy-start | bytes 1572868
  74.1 17.8 %copy-start.21 = (bf16[1024,256]{0,1:T(8,128)(2,1)}, bf16[1024,256]{0,1:T(8,128)(2,1)S(1)}, u32[]{:S(2)}) copy-start(bf16[1024,256]{0,1:T(8,128)(2,1)S(1)} %get-tuple-element.56) | copy-start | bytes 1572868
  91.9 9.2 %copy-start.29 = (bf16[256,1024]{1,0:T(8,128)(2,1)S(1)}, bf16[256,1024]{1,0:T(8,128)(2,1)}, u32[]{:S(2)}) copy-start(bf16[256,1024]{1,0:T(8,128)(2,1)} %param.20) | copy-start | bytes 1572868
  147.8 1.0 copy-start.11
  182.2 1.3 copy-start.6
  183.6 2.2 copy-start.7
  185.5 12.6 %copy-start.22 = (bf16[4,8,32,1024]{3,2,1,0:T(8,128)(2,1)}, bf16[4,8,32,1024]{3,2,1,0:T(8,128)(2,1)S(1)}, u32[]{:S(2)}) copy-start(bf16[4,8,32,1024]{3,2,1,0:T(8,128)(2,1)S(1)} %copy.76) | copy-start | bytes 6291460
  198.2 1.3 copy-start.42
  199.5 50.6 %copy-start.12 = (f32[256,1024]{1,0:T(8,128)S(1)}, f32[256,1024]{1,0:T(8,128)}, u32[]{:S(2)}) copy-start(f32[256,1024]{1,0:T(8,128)} %copy-done.11) | copy-start | bytes 3145732
  201.8 48.9 %copy-start.19 = (bf16[256,1024]{1,0:T(8,128)(2,1)S(1)}, bf16[256,1024]{1,0:T(8,128)(2,1)}, u32[]{:S(2)}) copy-start(bf16[256,1024]{1,0:T(8,128)(2,1)} %param.31) | copy-start | bytes 1572868
  250.5 1.0 copy-start.13
  251.5 28.9 %copy-start.44 = (f32[1024,1024]{1,0:T(8,128)S(1)}, f32[1024,1024]{1,0:T(8,128)}, u32[]{:S(2)}) copy-start(f32[1024,1024]{1,0:T(8,128)} %get-tuple-element.52) | copy-start | bytes 12582916
  280.4 12.6 %copy-start.3 = (bf16[1024,1024]{1,0:T(8,128)(2,1)}, bf16[1024,1024]{1,0:T(8,128)(2,1)S(1)}, u32[]{:S(2)}) copy-start(bf16[1024,1024]{1,0:T(8,128)(2,1)S(1)} %get-tuple-element.27) | copy-start | bytes 6291460
  280.4 6.4 %copy-start.8 = (bf16[1024,1024]{1,0:T(8,128)(2,1)S(1)}, bf16[1024,1024]{1,0:T(8,128)(2,1)}, u32[]{:S(2)}) copy-start(bf16[1024,1024]{1,0:T(8,128)(2,1)} %copy-done.6) | copy-start | bytes 6291460
  286.8 3.8 copy-start.23
  290.6 2.4 copy-start.43
  374.2 3.7 copy-start.10
  377.4 147.3 %all-reduce.10.cloned.1.call-start = ((), (), s32[]{:S(2)}) async-start(), calls=%async_computation.4 | async-start | bytes 4259840 | tf_op jit(solution)/shard_map/psum | solution.py:449
  390.7 16.2 %copy-start.28 = (bf16[1024,256]{0,1:T(8,128)(2,1)S(1)}, bf16[1024,256]{0,1:T(8,128)(2,1)}, u32[]{:S(2)}) copy-start(bf16[1024,256]{0,1:T(8,128)(2,1)} %convolution_convert_fusion.10) | copy-start | bytes 1572868
  421.1 2.8 copy-start.18
  423.9 7.1 %copy-start.31 = (bf16[4,64,1024]{2,1,0:T(8,128)(2,1)S(1)}, bf16[4,64,1024]{2,1,0:T(8,128)(2,1)}, u32[]{:S(2)}) copy-start(bf16[4,64,1024]{2,1,0:T(8,128)(2,1)} %get-tuple-element.78) | copy-start | bytes 1572868
  423.9 33.9 %copy-start.5 = (bf16[1024,1024]{1,0:T(8,128)(2,1)S(1)}, bf16[1024,1024]{1,0:T(8,128)(2,1)}, u32[]{:S(2)}) copy-start(bf16[1024,1024]{1,0:T(8,128)(2,1)} %copy-done.4) | copy-start | bytes 6291460
  461.1 72.2 %copy-start.25 = (bf16[4,64,1024]{2,1,0:T(8,128)(2,1)S(1)}, bf16[4,64,1024]{2,1,0:T(8,128)(2,1)}, u32[]{:S(2)}) copy-start(bf16[4,64,1024]{2,1,0:T(8,128)(2,1)} %copy-done.24) | copy-start | bytes 1572868
  462.4 130.4 %all-gather.15.cloned.1.call-start = ((), (), s32[]{:S(2)}) async-start(), calls=%async_computation.3 | async-start | bytes 2359296 | tf_op jit(solution)/shard_map/all_gather | solution.py:396
  472.9 130.5 %all-gather.13.cloned.1.call-start = ((), (), s32[]{:S(2)}) async-start(), calls=%async_computation.2 | async-start | bytes 1769472 | tf_op jit(solution)/shard_map/all_gather | solution.py:396
  533.3 53.1 %copy-start.15 = (f32[256,1024]{1,0:T(8,128)S(1)}, f32[256,1024]{1,0:T(8,128)}, u32[]{:S(2)}) copy-start(f32[256,1024]{1,0:T(8,128)} %copy-done.14) | copy-start | bytes 3145732
  536.9 50.5 %copy-start.20 = (bf16[1040,1024]{1,0:T(8,128)(2,1)S(1)}, bf16[1040,1024]{1,0:T(8,128)(2,1)}, u32[]{:S(2)}) copy-start(bf16[1040,1024]{1,0:T(8,128)(2,1)} %get-tuple-element.32) | copy-start | bytes 6389764
  586.4 4.6 copy-start.27
  609.0 11.2 %copy-start.1 = (bf16[1024,1024]{1,0:T(8,128)(2,1)S(1)}, bf16[1024,1024]{1,0:T(8,128)(2,1)}, u32[]{:S(2)}) copy-start(bf16[1024,1024]{1,0:T(8,128)(2,1)} %param.26) | copy-start | bytes 6291460
  (3 other events, 2.6 us)
Sparse Core Ops, SparseCore 0:
  24.4 28.1 all-gather.8
  55.0 27.8 all-gather.10
  377.6 80.2 all-reduce.11
  462.5 62.1 all-reduce.9
  526.6 27.0 all-gather.14
  555.6 25.6 all-gather.12

commit v3 on v2

--- a/solution.py
+++ b/solution.py
@@ -32,6 +32,12 @@
 
 MESH = pl.DeviceIdType.MESH
 EXTRA = 16
+
+
+def cost(micros):
+    return pl.CostEstimate(
+        flops=micros * 10**9, bytes_accessed=micros * 3 * 10**6, transcendentals=0
+    )
 
 
 def greet_neighbours(me, n):
@@ -114,7 +120,7 @@
                     copy(way, block, at).wait_send()
 
 
-def gather_rows(rows, extra, place):
+def gather_rows(rows, extra, place, micros=25):
     n = lax.axis_size("group")
     cuts = chunk_rows(rows.shape[0], 4)
     vmem = pl.BlockSpec(memory_space=pltpu.VMEM)
@@ -133,93 +139,95 @@
         compiler_params=pltpu.CompilerParams(
             collective_id=place, has_side_effects=True, vmem_limit_bytes=40 * 2**20
         ),
+        cost_estimate=cost(micros),
     )(rows, extra)
 
 
-def reduce_kernel(n, cuts, x_ref, out_ref, right_ref, left_ref, send_sem, recv_sem):
+def reduce_kernel(n, cuts, lag, x_ref, out_ref, held_ref, send_sem, recv_sem):
     me = lax.axis_index("group")
     rows = out_ref.shape[0]
+    near = jnp.where(me < n // 2, 0, 1)
+    size = cuts[0][1]
     greet_neighbours(me, n)
 
     def copy(way, block, at):
-        start, size = cuts[at]
-        ref = right_ref if way == 0 else left_ref
-        part = ref.at[block, pl.ds(start, size)]
-        target = me + 1 if way == 0 else me - 1
+        part = held_ref.at[way, block, pl.ds(cuts[at][0], size)]
+        target = me + 1 - 2 * way
         return remote(part, part, send_sem.at[way, block, at], recv_sem.at[way, block, at], target)
 
-    for step in range(n - 1):
-        for at, (start, size) in enumerate(cuts):
-            for way in range(2):
-                block = n - 1 - step if way == 0 else step
-                ref = right_ref if way == 0 else left_ref
-                first = me == 0 if way == 0 else me == n - 1
-                passes = me < block if way == 0 else me > block
-                mine = x_ref[block * rows + start : block * rows + start + size]
-
-                @pl.when(jnp.logical_and(passes, first))
-                def _():
-                    ref[block, start : start + size] = mine
-
-                @pl.when(jnp.logical_and(passes, jnp.logical_not(first)))
-                def _():
-                    copy(way, block, at).wait_recv()
-                    held = ref[block, start : start + size].astype(jnp.float32)
-                    ref[block, start : start + size] = (
-                        held + mine.astype(jnp.float32)
-                    ).astype(ref.dtype)
-
-                @pl.when(passes)
-                def _():
-                    copy(way, block, at).start()
-
-    for at, (start, size) in enumerate(cuts):
+    def place(way, step):
+        block = jnp.where(way == 0, n - 1 - step, step)
+        first = me == jnp.where(way == 0, 0, n - 1)
+        ahead = jnp.where(way == 0, block - me, me - block)
+        return block, first, ahead > 0
+
+    def send(way, step, at):
+        block, first, passes = place(way, step)
+        start = cuts[at][0]
+        here = pl.ds(start, size)
+        mine = pl.ds(pl.multiple_of(block * rows + start, 16), size)
+
+        @pl.when(jnp.logical_and(passes, first))
+        def _():
+            held_ref[way, block, here] = x_ref[mine]
+
+        @pl.when(jnp.logical_and(passes, jnp.logical_not(first)))
+        def _():
+            copy(way, block, at).wait_recv()
+            held_ref[way, block, here] = (
+                held_ref[way, block, here].astype(jnp.float32) + x_ref[mine].astype(jnp.float32)
+            ).astype(held_ref.dtype)
+
+        @pl.when(passes)
+        def _():
+            copy(way, block, at).start()
+
+    items = [(step, at) for step in range(n - 1) for at in range(len(cuts))]
+    for now in range(len(items) + lag):
+        if now < len(items):
+            send(near, *items[now])
+        if now >= lag:
+            send(1 - near, *items[now - lag])
+
+    for at, (start, _) in enumerate(cuts):
+        here = pl.ds(start, size)
         own = pl.ds(pl.multiple_of(me * rows + start, 16), size)
-        out_ref[start : start + size] = x_ref[own].astype(jnp.float32)
-
-        @pl.when(me > 0)
-        def _():
-            copy(0, me, at).wait_recv()
-            out_ref[start : start + size] += right_ref[me, start : start + size].astype(
-                jnp.float32
-            )
-
-        @pl.when(me < n - 1)
-        def _():
-            copy(1, me, at).wait_recv()
-            out_ref[start : start + size] += left_ref[me, start : start + size].astype(
-                jnp.float32
-            )
-
-    for step in range(n - 1):
-        for at in range(len(cuts)):
-            for way in range(2):
-                block = n - 1 - step if way == 0 else step
-
-                @pl.when(me < block if way == 0 else me > block)
-                def _():
-                    copy(way, block, at).wait_send()
-
-
-def reduce_rows(terms, place):
+        out_ref[here] = x_ref[own].astype(jnp.float32)
+        for way in range(2):
+
+            @pl.when(me > 0 if way == 0 else me < n - 1)
+            def _():
+                copy(way, me, at).wait_recv()
+                out_ref[here] += held_ref[way, me, here].astype(jnp.float32)
+
+    for step, at in items:
+        for way in range(2):
+            block, _, passes = place(way, step)
+
+            @pl.when(passes)
+            def _():
+                copy(way, block, at).wait_send()
+
+
+def reduce_rows(terms, place, micros=25):
     n = lax.axis_size("group")
     rows, width = terms.shape[0] // n, terms.shape[1]
     cuts = chunk_rows(rows, 4)
     vmem = pl.BlockSpec(memory_space=pltpu.VMEM)
     return pl.pallas_call(
-        functools.partial(reduce_kernel, n, cuts),
+        functools.partial(reduce_kernel, n, cuts, 3),
         out_shape=jax.ShapeDtypeStruct((rows, width), jnp.float32),
         in_specs=[vmem],
         out_specs=vmem,
         scratch_shapes=[
-            pltpu.VMEM((n, rows, width), jnp.bfloat16),
-            pltpu.VMEM((n, rows, width), jnp.bfloat16),
+            pltpu.VMEM((2, n, rows, width), jnp.bfloat16),
             pltpu.SemaphoreType.DMA((2, n, len(cuts))),
             pltpu.SemaphoreType.DMA((2, n, len(cuts))),
         ],
         compiler_params=pltpu.CompilerParams(
             collective_id=place, has_side_effects=True, vmem_limit_bytes=40 * 2**20
         ),
+        cost_estimate=cost(micros),
     )(terms.astype(jnp.bfloat16))
 
 
@@ -268,6 +276,7 @@
         compiler_params=pltpu.CompilerParams(
             collective_id=place, has_side_effects=True, vmem_limit_bytes=40 * 2**20
         ),
+        cost_estimate=cost(8),
     )(parts)
 
 
@@ -386,28 +395,36 @@
         [own_sums(second_extra).reshape(-1), own_columns(outer_all), inner_bias_grad], D
     )
     inner_weight_grad = matmul(first_all.T, inner_grad).astype(jnp.bfloat16)
+    outer_weight_grad = jnp.concatenate([outer_weight_grad, early], axis=0)
+    outer_weight_grad, inner_weight_grad, later_grad = lax.optimization_barrier(
+        (outer_weight_grad, inner_weight_grad, inner_grad)
+    )
     outer_weight_grad, inner_weight_grad = lax.psum(
-        (jnp.concatenate([outer_weight_grad, early], axis=0), inner_weight_grad), "replica"
-    )
-
-    def to_rows(columns, place):
-        parts = columns.reshape(groups, replicas, piece, columns.shape[-1])
+        (outer_weight_grad, inner_weight_grad), "replica"
+    )
+
+    def to_rows(columns, sections, place):
+        width = columns.shape[-1]
+        parts = columns.reshape(groups, replicas, piece, width)
         parts = lax.dynamic_index_in_dim(parts, replica_place, axis=1, keepdims=False)
-        return lax.all_gather(exchange(parts, place), "replica", axis=0)
-
-    inner_rows_grad = to_rows(inner_weight_grad, 6)
-    inner_rows_grad = inner_rows_grad.transpose(0, 2, 1, 3).reshape(own, groups * hidden)
-    inner_rows_grad = inner_rows_grad.astype(jnp.float32)
-    first_grad = second_res_grad + reduce_rows(matmul(inner_grad, inner_cols.T), 7)
+        parts = exchange(parts, place).reshape(groups, piece, sections, width // sections)
+        parts = parts.transpose(1, 2, 0, 3).reshape(piece, groups * width)
+        whole_rows = lax.all_gather(parts, "replica", axis=0, tiled=True)
+        return whole_rows.astype(jnp.float32)
+
+    first_grad = second_res_grad + reduce_rows(matmul(later_grad, inner_cols.T), 7, 0)
 
     first_res_grad, first_gain_grad, first_shift_grad = first_pull(first_grad)
     branch_grad = first_res_grad.astype(jnp.bfloat16)
     branch_all, first_extra = gather_rows(
-        branch_grad, extra_rows([first_gain_grad, first_shift_grad], D), 8
+        branch_grad, extra_rows([first_gain_grad, first_shift_grad], D), 8, 0
     )
     attended_grad = matmul(branch_all, attn_weight.T).astype(jnp.bfloat16)
+    attended_grad, inner_weight_grad, outer_weight_grad, branch_all = lax.optimization_barrier(
+        (attended_grad, inner_weight_grad, outer_weight_grad, branch_all)
+    )
+    attn_weight_grad = matmul(attended.T, branch_all).astype(jnp.bfloat16)
     attended_grad = attended_grad.reshape(length, heads, HD)
-    attn_weight_grad = matmul(attended.T, branch_all).astype(jnp.bfloat16)
 
     probs = jnp.exp(masked_scores() - log_total)
     probs_low = probs.astype(jnp.bfloat16)
@@ -442,21 +459,19 @@
         D,
     )
     attn_weight_grad = jnp.concatenate([attn_weight_grad, late], axis=0)
-    last_grad, _, outer_weight_grad = lax.optimization_barrier(
-        (projected_grad, inner_weight_grad, outer_weight_grad)
-    )
-    qkv_weight_grad = matmul(input_all.T, last_grad).astype(jnp.bfloat16)
+    inner_rows_grad = to_rows(inner_weight_grad, 1, 6)
+    qkv_weight_grad = matmul(input_all.T, projected_grad).astype(jnp.bfloat16)
     qkv_weight_grad, attn_weight_grad = lax.psum((qkv_weight_grad, attn_weight_grad), "replica")
     input_terms = reduce_rows(matmul(projected_grad, qkv_cols.T), 9)
     input_grad = (first_res_grad + input_terms).astype(jnp.bfloat16)
     early = outer_weight_grad[hidden:].reshape(-1).astype(jnp.float32)
     outer_weight_grad = outer_weight_grad[:hidden].astype(jnp.float32)
+    qkv_weight_grad, attn_weight_grad, input_grad = lax.optimization_barrier(
+        (qkv_weight_grad, attn_weight_grad, input_grad)
+    )
     late = attn_weight_grad[own:].reshape(-1).astype(jnp.float32)
     attn_weight_grad = attn_weight_grad[:own].astype(jnp.float32)
-    qkv_weight_grad = to_rows(qkv_weight_grad, 10)
-    qkv_weight_grad = qkv_weight_grad.reshape(replicas, groups, piece, 3, own)
-    qkv_weight_grad = qkv_weight_grad.transpose(0, 2, 3, 1, 4).reshape(own, 3 * D)
-    qkv_weight_grad = qkv_weight_grad.astype(jnp.float32)
+    qkv_weight_grad = to_rows(qkv_weight_grad, 3, 10)
     second_gain_grad, second_shift_grad, outer_bias_grad = early[: 3 * own].reshape(3, own)
     inner_bias_grad = early[3 * own : 3 * own + hidden]
     late = late[: 5 * own].reshape(5, own)

time: 639 us -> 556 us (0.87)
  Pallas kernels: 344 us -> 314 us
  waiting for transfers between devices: 77.3 us -> 50.3 us
  local copies, waits for them, and re-layouts: 47.1 us -> 23.8 us
  matrix products: 95.8 us -> 89.4 us
    pallas_call x4, Pallas kernels: 189 us -> 134 us  [reduce_rows(): pl.pallas_call(functools.partial(reduce_kernel, n, cuts, 3), out_shape=ja...]
    psum x1, waiting for transfers between devices: 51.6 us -> 10.3 us  [on_device(): lax.psum((qkv_weight_grad, attn_weight_grad), 'replica')]
    all_gather x2, waiting for transfers between devices: 0.01 us -> 37.5 us  [to_rows(): whole_rows = lax.all_gather(parts, 'replica', axis=0, tiled=True)]
    pallas_call x4, Pallas kernels: 124 us -> 151 us  [gather_rows(): pl.pallas_call(functools.partial(gather_kernel, n, cuts), out_shape=[jax....]
    psum x1, waiting for transfers between devices: 25.5 us -> 2.47 us  [on_device(): lax.psum((outer_weight_grad, inner_weight_grad), 'replica')]
    convert_element_type x4 -> x0, local copies, waits for them, and re-layouts: 19.5 us -> none  [the longest x3 16.8 us: on_device(): qkv_weight_grad = qkv_weight_grad.astype(jnp.float32)]
    unnamed x96 -> x109, local copies, waits for them, and re-layouts: 14.9 us -> 9.58 us
  transfers between devices with their start and end apart: 6 -> 6, of which waited for: 2 -> 4; matrix products, arithmetic and copies ran while one was open for 18% -> 12% of each run, Pallas kernels for 29% -> 42%
where the time goes in v3:
time: 556 us; the launch traced here: 546 us
  Pallas kernels  314 us (56%)
  matrix products  89.4 us (16%)
  other arithmetic  52.1 us (9%)
  waiting for transfers between devices  50.3 us (9%)
  local copies, waits for them, and re-layouts  23.8 us (4%)
  between operations  15.6 us (3%)
    pallas_call x4, Pallas kernels, gather_rows(): pl.pallas_call(functools.partial(gather_kernel, n, cuts), out_shape=[jax....  151 us
    pallas_call x4, Pallas kernels, reduce_rows(): pl.pallas_call(functools.partial(reduce_kernel, n, cuts, 3), out_shape=ja...  134 us
    dot_general x12, matrix products, matmul(): return jnp.dot(left, right, preferred_element_type=jnp.float32)  46.9 us
    all_gather x2, waiting for transfers between devices, to_rows(): whole_rows = lax.all_gather(parts, 'replica', axis=0, tiled=True)  37.5 us
    pallas_call x3, Pallas kernels, exchange(): pl.pallas_call(functools.partial(exchange_kernel, n), out_shape=jax.Shape...  29.2 us
    convert_element_type x1, other arithmetic, on_device(): scores_grad = (probs * (probs_grad - weighted)).astype(jnp.bfloat16)  12 us
    dot_general x1, matrix products, on_device(): jnp.einsum('qhd,khd->hqk', attended_grad, value_heads, preferred_element_...  12 us
  transfers between devices with their start and end apart: 6, of which 4 were waited for; matrix products, arithmetic and copies ran while one was open for 12% of the time, Pallas kernels for 42%

profile of v3, /device:TPU:0, one launch (start us, length us, event | category | flops | bytes accessed | tf_op | source)
XLA Modules:
  0.0 546.1 jit_solution(9461833552647154346)
XLA Ops:
  10.0 13.5 %shard_map.272 = bf16[4,32,1792]{2,1,0:T(8,128)(2,1)S(1)} custom-call(bf16[4,32,1792]{2,1,0:T(8,128)(2,1)S(1)} %pad_maximum_fusion.5.x_ref), custom_call_target="tpu_custom_call" | custom-call | flops 8000000000 | bytes 24000000 | tf_op jit(solution)/shard_map/pallas_call | solution.py:270
  25.2 1.6 broadcast_compare_fusion
  26.9 38.7 %shard_map.271 = (bf16[1024,1024]{1,0:T(8,128)(2,1)S(1)}, bf16[64,256]{1,0:T(8,128)(2,1)S(1)}) custom-call(bf16[256,1024]{1,0:T(8,128)(2,1)S(1)} %copy-done.1, bf16[16,256]{1,0:T(8,128)(2,1)S(1)} %pad.19.y_ref), custom_call_target="tpu_custom_call" | custom-call | flops 24999999488 | bytes 75000000 | tf_op jit(solution)/shard_map/pallas_call | solution.py:127
  65.6 1.4 copy-done.4
  68.3 1.5 copy.78
  69.9 4.0 fusion.62
  74.3 1.4 copy-done.8
  75.7 7.4 %select_reduce_fusion = (f32[4,1024]{1,0:T(4,128)S(1)}, f32[4,1024,1024]{1,2,0:T(8,128)}) fusion(pred[1024,1024]{0,1:T(8,128)(4,1)S(1)} %copy-done.8, bf16[1024,4,64]{0,2,1:T(8,128)(2,1)S(1)} %bitcast.112, bf16[1024,4,64]{0,2,1:T(8,128)(2,1)S(1)} %bitcast.110), kind=kOutput, calls=%fused_computation.6 | convolution fusion | flops 545255424 | bytes 18890752 | tf_op jit(solution)/shard_map/qhd,khd->hqk/dot_general | solution.py:342
  83.1 9.0 %fusion = f32[4,1024]{1,0:T(4,128)S(1)} fusion(f32[4,1024,1024]{1,2,0:T(8,128)} %get-tuple-element.89, f32[4,1024]{1,0:T(4,128)S(1)} %get-tuple-element.88, pred[1024,1024]{0,1:T(8,128)(4,1)} %broadcast_compare_fusion), kind=kLoop, calls=%fused_computation.5 | loop fusion | flops 12578816 | bytes 17858560 | tf_op jit(solution)/shard_map/reduce_sum | solution.py:348
  92.1 8.4 %fusion.18 = bf16[4,64,1024]{2,1,0:T(8,128)(2,1)S(1)} fusion(bf16[1024,4,64]{0,2,1:T(8,128)(2,1)S(1)} %bitcast.116, f32[4,1024,1024]{1,2,0:T(8,128)} %get-tuple-element.89, f32[4,1024]{1,0:T(4,128)S(1)} %fusion, f32[4,1024]{1,0:T(4,128)S(1)} %get-tuple-element.88, pred[1024,1024]{0,1:T(8,128)(4,1)} %broadcast_compare_fusion), kind=kOutput, calls=%fused_computation.51 | convolution fusion | flops 553910272 | bytes 18907136 | tf_op jit(solution)/shard_map/hqk,khd->qhd/dot_general | solution.py:351
  102.1 34.1 %shard_map.273 = f32[256,1024]{1,0:T(8,128)S(1)} custom-call(bf16[1024,1024]{1,0:T(8,128)(2,1)S(1)} %convolution_convert_fusion.4.x_ref), custom_call_target="tpu_custom_call" | custom-call | flops 24999999488 | bytes 75000000 | tf_op jit(solution)/shard_map/pallas_call | solution.py:217
  137.4 37.8 %shard_map.274 = (bf16[1024,1024]{1,0:T(8,128)(2,1)S(1)}, bf16[64,128]{1,0:T(8,128)(2,1)}) custom-call(bf16[256,1024]{1,0:T(8,128)(2,1)S(1)} %fusion.26.x_ref, bf16[16,128]{1,0:T(8,128)(2,1)S(1)} %broadcast_in_dim.28.y_ref), custom_call_target="tpu_custom_call" | custom-call | flops 24999999488 | bytes 75000000 | tf_op jit(solution)/shard_map/pallas_call | solution.py:127
  176.6 1.9 copy.80
  178.8 12.3 %multiply_convert_fusion.1 = (bf16[1024,1024]{1,0:T(8,128)(2,1)S(1)}, f32[1024,1024]{1,0:T(8,128)}, f32[1024,1024]{1,0:T(8,128)}) fusion(f32[1024]{0:T(1024)S(1)} %convert_element_type.265, bf16[1024,1024]{1,0:T(8,128)(2,1)S(1)} %copy-done.6, bf16[1024,1024]{1,0:T(8,128)(2,1)S(1)} %bitcast.119), kind=kOutput, calls=%fused_computation.14 | convolution fusion | flops 2216689664 | bytes 14684160 | tf_op jit(solution)/shard_map/dot_general | solution.py:30
  192.4 2.3 convolution_convert_fusion.3.x_ref
  194.8 32.5 %shard_map.275 = f32[256,1024]{1,0:T(8,128)S(1)} custom-call(bf16[1024,1024]{1,0:T(8,128)(2,1)S(1)} %convolution_convert_fusion.3.x_ref), custom_call_target="tpu_custom_call" | custom-call | flops 24999999488 | bytes 75000000 | tf_op jit(solution)/shard_map/pallas_call | solution.py:217
  228.8 1.6 fusion.55
  231.8 38.6 %shard_map.276 = (bf16[1024,1024]{1,0:T(8,128)(2,1)S(1)}, bf16[64,1024]{1,0:T(8,128)(2,1)S(1)}) custom-call(bf16[256,1024]{1,0:T(8,128)(2,1)S(1)} %add_convert_fusion.4.x_ref, bf16[16,1024]{1,0:T(8,128)(2,1)S(1)} %reshape.309.y_ref), custom_call_target="tpu_custom_call" | custom-call | flops 24999999488 | bytes 75000000 | tf_op jit(solution)/shard_map/pallas_call | solution.py:127
  270.4 3.7 convolution_convert_fusion.2
  274.1 4.1 fusion.54
  278.2 3.8 convolution_convert_fusion.1
  282.2 3.1 pad_maximum_fusion
  285.4 4.7 convolution_convert_fusion.x_ref
  290.1 31.0 %shard_map.277 = f32[256,1024]{1,0:T(8,128)S(1)} custom-call(bf16[1024,1024]{1,0:T(8,128)(2,1)S(1)} %convolution_convert_fusion.x_ref), custom_call_target="tpu_custom_call" | custom-call | tf_op jit(solution)/shard_map/pallas_call | solution.py:217
  321.1 1.4 multiply_reduce_fusion.1
  322.6 1.7 fusion.53
  324.4 36.1 %shard_map.278 = (bf16[1024,1024]{1,0:T(8,128)(2,1)S(1)}, bf16[64,1024]{1,0:T(8,128)(2,1)S(1)}) custom-call(bf16[256,1024]{1,0:T(8,128)(2,1)S(1)} %add_convert_fusion.3.x_ref, bf16[16,1024]{1,0:T(8,128)(2,1)S(1)} %reshape.313.y_ref), custom_call_target="tpu_custom_call" | custom-call | tf_op jit(solution)/shard_map/pallas_call | solution.py:127
  361.9 1.6 convolution_convert_fusion.10
  363.4 2.5 all-reduce.12.cloned.1.call-done
  365.9 2.0 copy.81
  367.9 12.0 %multiply_reduce_fusion = (f32[4,1024]{1,0:T(4,128)S(1)}, f32[4,1024,1024]{1,2,0:T(8,128)}) fusion(f32[4,1024,1024]{1,2,0:T(8,128)} %get-tuple-element.89, f32[4,1024]{1,0:T(4,128)S(1)} %log_add_fusion, pred[1024,1024]{0,1:T(8,128)(4,1)S(1)} %copy-done.9, bf16[1024,4,64]{0,2,1:T(8,128)(2,1)} %bitcast.114, bf16[1024,4,64]{0,2,1:T(8,128)(2,1)} %bitcast.117), kind=kOutput, calls=%fused_computation.1 | convolution fusion | flops 553644032 | bytes 35684352 | tf_op jit(solution)/shard_map/qhd,khd->hqk/dot_general | solution.py:431
  380.0 12.0 %multiply_convert_fusion = bf16[4,1024,1024]{1,2,0:T(8,128)(2,1)S(1)} fusion(f32[4,1024,1024]{1,2,0:T(8,128)} %get-tuple-element.92, f32[4,1024,1024]{1,2,0:T(8,128)} %get-tuple-element.89, f32[4,1024]{1,0:T(4,128)S(1)} %get-tuple-element.91, f32[4,1024]{1,0:T(4,128)S(1)} %log_add_fusion, pred[1024,1024]{0,1:T(8,128)(4,1)S(1)} %copy-done.9), kind=kLoop, calls=%fused_computation | loop fusion | flops 20971520 | bytes 43024384 | tf_op jit(solution)/shard_map/convert_element_type | solution.py:438
  392.0 2.4 bitcast_reduce_fusion
  394.4 3.5 convolution_convert_fusion.7
  397.9 8.9 %fusion.61 = (bf16[4,64]{1,0:T(4,128)(2,1)S(1)}, bf16[4,64,1024]{2,1,0:T(8,128)(2,1)}) fusion(bf16[1024,4,64]{0,2,1:T(8,128)(2,1)S(1)} %bitcast.115, f32[4,1024,1024]{1,2,0:T(8,128)} %get-tuple-element.89, f32[4,1024]{1,0:T(4,128)S(1)} %log_add_fusion, pred[1024,1024]{0,1:T(8,128)(4,1)S(1)} %copy-done.9), kind=kOutput, calls=%fused_computation.144 | convolution fusion | flops 549977856 | bytes 18891264 | tf_op jit(solution)/shard_map/hqk,qhd->khd/dot_general | solution.py:434
  406.8 1.5 convolution_convert_fusion.9
  408.7 1.9 pad_maximum_fusion.4
  410.6 4.7 convolution_convert_fusion.6
  416.3 8.7 %shard_map.281 = bf16[4,32,1024]{2,1,0:T(8,128)(2,1)S(1)} custom-call(bf16[4,32,1024]{2,1,0:T(8,128)(2,1)S(1)} %dynamic-slice_bitcast_fusion.x_ref), custom_call_target="tpu_custom_call" | custom-call | flops 8000000000 | bytes 24000000 | tf_op jit(solution)/shard_map/pallas_call | solution.py:270
  426.4 3.5 convolution_convert_fusion.5.x_ref
  429.9 36.4 %shard_map.279 = f32[256,1024]{1,0:T(8,128)S(1)} custom-call(bf16[1024,1024]{1,0:T(8,128)(2,1)S(1)} %convolution_convert_fusion.5.x_ref), custom_call_target="tpu_custom_call" | custom-call | flops 24999999488 | bytes 75000000 | tf_op jit(solution)/shard_map/pallas_call | solution.py:217
  467.2 10.3 %all-reduce.10.cloned.1.call-done = (bf16[1024,768]{1,0:T(8,128)(2,1)}, bf16[272,1024]{1,0:T(8,128)(2,1)}) async-done(((bf16[1024,768]{1,0:T(8,128)(2,1)}, bf16[272,1024]{1,0:T(8,128)(2,1)}), (bf16[1024,768]{1,0:T(8,128)(2,1)}, bf16[272,1024]{1,0:T(8,128)(2,1)})) %all-reduce.10.cloned.1.call-update) | async-done | bytes 2129936 | tf_op jit(solution)/shard_map/psum | solution.py:464
  478.5 7.0 %shard_map.280 = bf16[4,32,768]{2,1,0:T(8,128)(2,1)S(1)} custom-call(bf16[4,32,768]{2,1,0:T(8,128)(2,1)S(1)} %dynamic-slice_bitcast_fusion.1.x_ref), custom_call_target="tpu_custom_call" | custom-call | flops 8000000000 | bytes 24000000 | tf_op jit(solution)/shard_map/pallas_call | solution.py:270
  488.0 4.1 slice_convert_fusion
  493.8 13.4 %all-gather.9.cloned.1.call-done = bf16[256,4096]{1,0:T(8,128)(2,1)} async-done(((bf16[32,4096]{1,0:T(8,128)(2,1)}), bf16[256,4096]{1,0:T(8,128)(2,1)}) %all-gather.9.cloned.1.call-update) | async-done | bytes 2097168 | tf_op jit(solution)/shard_map/all_gather | solution.py:412
  507.1 4.1 convert_element_type.309
  511.2 24.1 %all-gather.7.cloned.1.call-done = bf16[256,3072]{1,0:T(8,128)(2,1)} async-done(((bf16[32,3072]{1,0:T(8,128)(2,1)}), bf16[256,3072]{1,0:T(8,128)(2,1)}) %all-gather.7.cloned.1.call-update) | async-done | bytes 1572880 | tf_op jit(solution)/shard_map/all_gather | solution.py:412
  535.3 3.4 convert_element_type.305
  (191 shorter events, 25.0 us)
Async XLA Ops:
  7.2 185.2 %copy-start = (bf16[1024,1024]{1,0:T(8,128)(2,1)S(1)}, bf16[1024,1024]{1,0:T(8,128)(2,1)}, u32[]{:S(2)}) copy-start(bf16[1024,1024]{1,0:T(8,128)(2,1)} %param.26) | copy-start | bytes 6291460
  7.2 61.1 %all-gather.11.cloned.1.call-start = ((), (), s32[]{:S(2)}) async-start(), calls=%async_computation.2 | async-start | bytes 1769472 | tf_op jit(solution)/shard_map/all_gather | solution.py:319
  9.8 15.2 %copy-start.38 = (bf16[256]{0:T(256)(128)(2,1)S(1)}, bf16[256]{0:T(256)(128)(2,1)}, u32[]{:S(2)}) copy-start(bf16[256]{0:T(256)(128)(2,1)} %param.21) | copy-start | bytes 1540
  9.9 15.2 %copy-start.39 = (bf16[256]{0:T(256)(128)(2,1)S(1)}, bf16[256]{0:T(256)(128)(2,1)}, u32[]{:S(2)}) copy-start(bf16[256]{0:T(256)(128)(2,1)} %param.22) | copy-start | bytes 1540
  9.9 15.2 %copy-start.40 = (bf16[256]{0:T(256)(128)(2,1)S(1)}, bf16[256]{0:T(256)(128)(2,1)}, u32[]{:S(2)}) copy-start(bf16[256]{0:T(256)(128)(2,1)} %param.23) | copy-start | bytes 1540
  9.9 15.2 %copy-start.41 = (bf16[256]{0:T(256)(128)(2,1)S(1)}, bf16[256]{0:T(256)(128)(2,1)}, u32[]{:S(2)}) copy-start(bf16[256]{0:T(256)(128)(2,1)} %param.27) | copy-start | bytes 1540
  9.9 15.2 %copy-start.42 = (bf16[256]{0:T(256)(128)(2,1)S(1)}, bf16[256]{0:T(256)(128)(2,1)}, u32[]{:S(2)}) copy-start(bf16[256]{0:T(256)(128)(2,1)} %param.28) | copy-start | bytes 1540
  9.9 15.2 %copy-start.43 = (bf16[256]{0:T(256)(128)(2,1)S(1)}, bf16[256]{0:T(256)(128)(2,1)}, u32[]{:S(2)}) copy-start(bf16[256]{0:T(256)(128)(2,1)} %param.29) | copy-start | bytes 1540
  9.9 15.2 %copy-start.44 = (bf16[256]{0:T(256)(128)(2,1)S(1)}, bf16[256]{0:T(256)(128)(2,1)}, u32[]{:S(2)}) copy-start(bf16[256]{0:T(256)(128)(2,1)} %param.19) | copy-start | bytes 1540
  9.9 15.3 %copy-start.45 = (bf16[256]{0:T(256)(128)(2,1)S(1)}, bf16[256]{0:T(256)(128)(2,1)}, u32[]{:S(2)}) copy-start(bf16[256]{0:T(256)(128)(2,1)} %param.18) | copy-start | bytes 1540
  9.9 15.3 %copy-start.33 = (s32[1024]{0:T(1024)S(1)}, s32[1024]{0:T(1024)}, u32[]{:S(2)}) copy-start(s32[1024]{0:T(1024)} %param.30) | copy-start | bytes 12292
  10.0 16.9 %copy-start.1 = (bf16[256,1024]{1,0:T(8,128)(2,1)S(1)}, bf16[256,1024]{1,0:T(8,128)(2,1)}, u32[]{:S(2)}) copy-start(bf16[256,1024]{1,0:T(8,128)(2,1)} %x_ref.1) | copy-start | bytes 1572868
  24.2 152.4 %all-gather.13.cloned.1.call-start = ((), (), s32[]{:S(2)}) async-start(), calls=%async_computation.3 | async-start | bytes 2359296 | tf_op jit(solution)/shard_map/all_gather | solution.py:319
  25.0 340.9 %all-reduce.12.cloned.1.call-start = ((), (), s32[]{:S(2)}) async-start(), calls=%async_computation.5 | async-start | bytes 8454144 | tf_op jit(solution)/shard_map/psum | solution.py:402
  26.9 40.7 %copy-start.37 = (bf16[1024]{0:T(1024)(128)(2,1)S(1)}, bf16[1024]{0:T(1024)(128)(2,1)}, u32[]{:S(2)}) copy-start(bf16[1024]{0:T(1024)(128)(2,1)} %param.25) | copy-start | bytes 6148
  26.9 40.7 %copy-start.19 = (bf16[256,1024]{1,0:T(8,128)(2,1)S(1)}, bf16[256,1024]{1,0:T(8,128)(2,1)}, u32[]{:S(2)}) copy-start(bf16[256,1024]{1,0:T(8,128)(2,1)} %param.31) | copy-start | bytes 1572868
  69.8 4.1 copy-start.24
  73.9 1.7 copy-start.8
  74.0 9.1 %copy-start.15 = (bf16[1024,256]{0,1:T(8,128)(2,1)}, bf16[1024,256]{0,1:T(8,128)(2,1)S(1)}, u32[]{:S(2)}) copy-start(bf16[1024,256]{0,1:T(8,128)(2,1)S(1)} %slice.125) | copy-start | bytes 1572868
  74.2 8.8 %copy-start.17 = (bf16[1024,256]{0,1:T(8,128)(2,1)}, bf16[1024,256]{0,1:T(8,128)(2,1)S(1)}, u32[]{:S(2)}) copy-start(bf16[1024,256]{0,1:T(8,128)(2,1)S(1)} %get-tuple-element.71) | copy-start | bytes 1572868
  74.2 17.8 %copy-start.22 = (bf16[1024,256]{0,1:T(8,128)(2,1)}, bf16[1024,256]{0,1:T(8,128)(2,1)S(1)}, u32[]{:S(2)}) copy-start(bf16[1024,256]{0,1:T(8,128)(2,1)S(1)} %get-tuple-element.72) | copy-start | bytes 1572868
  92.1 9.2 %copy-start.28 = (bf16[256,1024]{1,0:T(8,128)(2,1)S(1)}, bf16[256,1024]{1,0:T(8,128)(2,1)}, u32[]{:S(2)}) copy-start(bf16[256,1024]{1,0:T(8,128)(2,1)} %param.20) | copy-start | bytes 1572868
  176.5 2.2 copy-start.6
  178.5 12.6 %copy-start.23 = (bf16[4,8,32,1024]{3,2,1,0:T(8,128)(2,1)}, bf16[4,8,32,1024]{3,2,1,0:T(8,128)(2,1)S(1)}, u32[]{:S(2)}) copy-start(bf16[4,8,32,1024]{3,2,1,0:T(8,128)(2,1)S(1)} %copy.80) | copy-start | bytes 6291460
  194.8 32.5 %copy-start.11 = (f32[256,1024]{1,0:T(8,128)S(1)}, f32[256,1024]{1,0:T(8,128)}, u32[]{:S(2)}) copy-start(f32[256,1024]{1,0:T(8,128)} %copy-done.10) | copy-start | bytes 3145732
  194.8 32.5 %copy-start.35 = (f32[1,4,256]{2,0,1:T(1,128)S(1)}, f32[1,4,256]{2,0,1:T(1,128)}, u32[]{:S(2)}) copy-start(f32[1,4,256]{2,0,1:T(1,128)} %get-tuple-element.84) | copy-start | bytes 12292
  227.3 3.1 copy-start.36
  231.8 38.6 %copy-start.47 = (bf16[1024,1024]{1,0:T(8,128)(2,1)S(1)}, bf16[1024,1024]{1,0:T(8,128)(2,1)}, u32[]{:S(2)}) copy-start(bf16[1024,1024]{1,0:T(8,128)(2,1)} %copy-done.46) | copy-start | bytes 6291460
  270.3 3.7 copy-start.48
  270.3 3.7 copy-start.49
  274.1 4.1 copy-start.7
  278.2 3.8 copy-start.50
  285.3 192.2 %all-reduce.10.cloned.1.call-start = ((), (), s32[]{:S(2)}) async-start(), calls=%async_computation.4 | async-start | bytes 4259840 | tf_op jit(solution)/shard_map/psum | solution.py:464
  285.4 35.7 %copy-start.14 = (f32[256,1024]{1,0:T(8,128)S(1)}, f32[256,1024]{1,0:T(8,128)}, u32[]{:S(2)}) copy-start(f32[256,1024]{1,0:T(8,128)} %get-tuple-element.64) | copy-start | bytes 3145732
  322.5 39.3 %copy-start.29 = (bf16[256,1024]{1,0:T(8,128)(2,1)S(1)}, bf16[256,1024]{1,0:T(8,128)(2,1)}, u32[]{:S(2)}) copy-start(bf16[256,1024]{1,0:T(8,128)(2,1)} %param.20) | copy-start | bytes 1572868
  324.3 36.3 %copy-start.12 = (f32[256,1024]{1,0:T(8,128)}, f32[256,1024]{1,0:T(8,128)S(1)}, u32[]{:S(2)}) copy-start(f32[256,1024]{1,0:T(8,128)S(1)} %get-tuple-element.59) | copy-start | bytes 3145732
  324.4 43.5 %copy-start.9 = (pred[1024,1024]{0,1:T(8,128)(4,1)S(1)}, pred[1024,1024]{0,1:T(8,128)(4,1)}, u32[]{:S(2)}) copy-start(pred[1024,1024]{0,1:T(8,128)(4,1)} %broadcast_compare_fusion) | copy-start | bytes 3145732
  380.0 12.1 %copy-start.16 = (bf16[1024,256]{0,1:T(8,128)(2,1)S(1)}, bf16[1024,256]{0,1:T(8,128)(2,1)}, u32[]{:S(2)}) copy-start(bf16[1024,256]{0,1:T(8,128)(2,1)} %copy-done.15) | copy-start | bytes 1572868
  392.0 2.4 copy-start.18
  394.4 3.5 copy-start.21
  397.9 8.9 %copy-start.3 = (bf16[1024,1024]{1,0:T(8,128)(2,1)S(1)}, bf16[1024,1024]{1,0:T(8,128)(2,1)}, u32[]{:S(2)}) copy-start(bf16[1024,1024]{1,0:T(8,128)(2,1)} %copy-done.2) | copy-start | bytes 6291460
  397.9 8.9 %copy-start.31 = (bf16[4,64,1024]{2,1,0:T(8,128)(2,1)S(1)}, bf16[4,64,1024]{2,1,0:T(8,128)(2,1)}, u32[]{:S(2)}) copy-start(bf16[4,64,1024]{2,1,0:T(8,128)(2,1)} %copy-done.30) | copy-start | bytes 1572868
  406.8 3.8 copy-start.26
  406.8 3.8 copy-start.27
  415.3 91.9 %all-gather.9.cloned.1.call-start = ((), (), s32[]{:S(2)}) async-start(), calls=%async_computation.1 | async-start | bytes 2359296 | tf_op jit(solution)/shard_map/all_gather | solution.py:412
  426.1 109.3 %all-gather.7.cloned.1.call-start = ((), (), s32[]{:S(2)}) async-start(), calls=%async_computation | async-start | bytes 1769472 | tf_op jit(solution)/shard_map/all_gather | solution.py:412
  429.8 36.4 %copy-start.13 = (f32[256,1024]{1,0:T(8,128)S(1)}, f32[256,1024]{1,0:T(8,128)}, u32[]{:S(2)}) copy-start(f32[256,1024]{1,0:T(8,128)} %copy-done.12) | copy-start | bytes 3145732
  485.5 6.6 %copy-start.25 = (bf16[272,1024]{1,0:T(8,128)(2,1)S(1)}, bf16[272,1024]{1,0:T(8,128)(2,1)}, u32[]{:S(2)}) copy-start(bf16[272,1024]{1,0:T(8,128)(2,1)} %get-tuple-element.46) | copy-start | bytes 1671172
  (9 other events, 10.7 us)
Sparse Core Ops, SparseCore 0:
  24.3 28.1 all-gather.10
  55.0 27.8 all-gather.12
  285.5 80.4 all-reduce.11
  415.4 62.1 all-reduce.9
  480.0 27.0 all-gather.8
  509.6 25.6 all-gather.6
